TPU v7x, 768 devices: a whole 4x8x12 slice. The times are simulated.
768 devices in a mesh: dp: 12 (over z_lo, core), expert: 64 (over x, z_hi, y).
Axes of the slice: x: 4, y: 8, z: 12 (z_hi: 2, z_lo: 6; z = z_hi * 6 + z_lo), core: 2. Of those that a mesh axis runs over, the one named last changes fastest.
Arguments:
- tokens: bfloat16 [16384, 6144], P('expert', 'dp'), may hold values from -6 to 6
- grad_out: bfloat16 [16384, 6144], P('expert', 'dp'), may hold values from -6 to 6
- expert_ids: int32 [16384, 2], P('expert'), may hold values from 0 to 319, as said below
- gates: float32 [16384, 2], P('expert'), may hold values from 0.1 to 1
- w_in: bfloat16 [64, 6144, 2048], P('expert', 'dp'), may hold values from -0.078125 to 0.078125
- w_out: bfloat16 [64, 1024, 6144], P('expert', None, 'dp'), may hold values from -0.1875 to 0.1875
Outputs:
- moe_out: bfloat16 [16384, 6144], P('expert', 'dp')
- grad_tokens: bfloat16 [16384, 6144], P('expert', 'dp')
Inputs may be any that keep to these rules, and one draw needn't show every extreme that they name: `expert_ids`: values of 64 or more name copy (identity) experts; every aligned block of 256 tokens holds exactly 128 entries under 64, and at most 3 of them name any one expert; in every draw one expert is named exactly 3 times in every block; a token's two entries may name the same expert.
All inputs are finite; a program needn't handle non-finite values.
Results may differ from a plain program's by a relative error of at most 0.017.
Values may be sent and summed in bfloat16 or wider, within the bound.
No kernel may reach another device: no remote copies, remote signals or barrier semaphores. Data moves between devices by JAX's collectives and lax.ppermute only.
A program may use at most 32 MiB of HBM per device.

v0:
```python
import jax
import jax.numpy as jnp
from jax import lax
from jax.sharding import PartitionSpec as P

CAP = 3


def finish(gate_up, hidden_grad, half):
    gate_part = gate_up[:, :half]
    up_part = gate_up[:, half:]
    sig = jax.nn.sigmoid(gate_part)
    silu = gate_part * sig
    dsilu = sig * (1.0 + gate_part * (1.0 - sig))
    hidden = (silu * up_part).astype(jnp.bfloat16)
    grads = jnp.concatenate([hidden_grad * up_part * dsilu, hidden_grad * silu], axis=1)
    return (hidden, grads.astype(jnp.bfloat16))


def per_device(tokens, grad_out, expert_ids, gates, w_in, w_out):
    n_dev = lax.axis_size("expert")
    width = tokens.shape[1]
    half = w_out.shape[1]
    tok_rows = tokens.shape[0]
    buffer_rows = n_dev * CAP
    flat_ids = expert_ids.reshape(2 * tok_rows)
    onehot = (flat_ids[:, None] == jnp.arange(n_dev, dtype=jnp.int32)[None, :]).astype(jnp.int32)
    before = jnp.cumsum(onehot, axis=0) - onehot
    rank = jnp.sum(before * onehot, axis=1).reshape(tok_rows, 2)
    slots = jnp.where(expert_ids < n_dev, rank, -1)
    row_index = jnp.arange(buffer_rows, dtype=jnp.int32)
    picker = ((row_index // CAP)[:, None, None] == expert_ids[None, :, :]) & (
        (row_index % CAP)[:, None, None] == slots[None, :, :]
    )
    picker = picker.astype(jnp.bfloat16)
    weighted_rows = (gates[:, :, None] * grad_out[:, None, :].astype(jnp.float32)).astype(
        jnp.bfloat16
    )
    send_rows = jnp.einsum("rtk,td->rd", picker, tokens, preferred_element_type=jnp.float32).astype(
        jnp.bfloat16
    )
    send_grads = jnp.einsum(
        "rtk,tkd->rd", picker, weighted_rows, preferred_element_type=jnp.float32
    ).astype(jnp.bfloat16)
    recv_rows, recv_grads = (
        lax.all_to_all(
            send_rows.reshape(n_dev, CAP, width), "expert", split_axis=0, concat_axis=0, tiled=True
        ),
        lax.all_to_all(
            send_grads.reshape(n_dev, CAP, width), "expert", split_axis=0, concat_axis=0, tiled=True
        ),
    )
    recv_rows = recv_rows.reshape(buffer_rows, width)
    recv_grads = recv_grads.reshape(buffer_rows, width)
    w_first = w_in[0]
    w_second = w_out[0]
    gate_part_sum = jnp.dot(recv_rows, w_first, preferred_element_type=jnp.float32)
    hidden_part_sum = jnp.einsum(
        "rd,fd->rf", recv_grads, w_second, preferred_element_type=jnp.float32
    )
    gate_up, hidden_grad = (
        lax.psum(gate_part_sum.astype(jnp.bfloat16), "dp").astype(jnp.float32),
        lax.psum(hidden_part_sum.astype(jnp.bfloat16), "dp").astype(jnp.float32),
    )
    hidden, gate_up_grad = finish(gate_up, hidden_grad, half)
    expert_out = jnp.dot(hidden, w_second, preferred_element_type=jnp.float32).astype(jnp.bfloat16)
    row_grad = jnp.einsum(
        "rf,df->rd", gate_up_grad, w_first, preferred_element_type=jnp.float32
    ).astype(jnp.bfloat16)
    back_out, back_grad = (
        lax.all_to_all(
            expert_out.reshape(n_dev, CAP, width), "expert", split_axis=0, concat_axis=0, tiled=True
        ),
        lax.all_to_all(
            row_grad.reshape(n_dev, CAP, width), "expert", split_axis=0, concat_axis=0, tiled=True
        ),
    )
    back_out = back_out.reshape(buffer_rows, width)
    back_grad = back_grad.reshape(buffer_rows, width)
    picked_out = jnp.einsum("rtk,rd->tkd", picker, back_out, preferred_element_type=jnp.float32)
    picked_grad = jnp.einsum("rtk,rd->tkd", picker, back_grad, preferred_element_type=jnp.float32)
    zero_route = (expert_ids >= n_dev).astype(jnp.float32)
    zero_weight = jnp.sum(gates * zero_route, axis=1)[:, None]
    moe_out = jnp.sum(gates[:, :, None] * picked_out, axis=1) + zero_weight * tokens.astype(
        jnp.float32
    )
    grad_tokens = jnp.sum(picked_grad, axis=1) + zero_weight * grad_out.astype(jnp.float32)
    return (moe_out.astype(jnp.bfloat16), grad_tokens.astype(jnp.bfloat16))


def solution(mesh):
    in_specs = (
        P("expert", "dp"),
        P("expert", "dp"),
        P("expert", None),
        P("expert", None),
        P("expert", "dp", None),
        P("expert", None, "dp"),
    )
    out_specs = (P("expert", "dp"), P("expert", "dp"))
    return jax.shard_map(
        per_device, mesh=mesh, in_specs=in_specs, out_specs=out_specs, check_vma=False
    )
```

profile of v0, /device:TPU:8, one launch (start us, length us, event | category | flops | bytes accessed | tf_op | source)
XLA Modules:
  0.0 289.9 jit_solution(411714255976858824)
XLA Ops:
  7.2 0.0 copy-start
  7.2 0.0 copy-start.7
  7.2 0.0 copy-start.8
  7.2 1.0 copy.17
  8.2 0.1 eq.61
  8.3 0.1 eq.57
  8.5 1.2 reduce-window.6
  9.7 0.2 slice_reduce_fusion
  10.0 0.0 copy-start.4
  10.0 0.1 fusion.21
  10.1 0.1 reshape.74
  10.2 0.1 copy.20
  10.3 0.7 compare_select_fusion.1
  11.0 1.0 convert_element_type.70
  12.0 0.0 copy-done.7
  12.0 0.0 copy-done.8
  12.0 0.4 fusion.4
  12.4 0.8 reshape.79
  13.2 23.2 %all-to-all-start.2 = ((bf16[64,3,512]{2,1,0:T(4,128)(2,1)}), bf16[64,3,512]{2,1,0:T(4,128)(2,1)S(1)}, u32[]{:S(2)}, u32[]{:S(2)}) async-start(bf16[64,3,512]{2,1,0:T(4,128)(2,1)} %reshape.79), calls=%async_computation.2 | async-start | bytes 524288 | tf_op jit(solution)/shard_map/all_to_all | solution.py:49
  36.5 0.1 convert_reduce_fusion
  36.6 0.0 copy-done.4
  36.6 0.2 fusion.29
  36.8 0.8 reshape.75
  37.7 15.7 %all-to-all-done.2 = bf16[64,3,512]{2,1,0:T(4,128)(2,1)S(1)} async-done(((bf16[64,3,512]{2,1,0:T(4,128)(2,1)}), bf16[64,3,512]{2,1,0:T(4,128)(2,1)S(1)}, u32[]{:S(2)}, u32[]{:S(2)}) %all-to-all-start.2) | async-done | bytes 196640 | tf_op jit(solution)/shard_map/all_to_all | solution.py:49
  53.4 7.5 %all-to-all-start = ((bf16[64,3,512]{2,1,0:T(4,128)(2,1)}), bf16[64,3,512]{2,1,0:T(4,128)(2,1)S(1)}, u32[]{:S(2)}, u32[]{:S(2)}) async-start(bf16[64,3,512]{2,1,0:T(4,128)(2,1)} %reshape.75), calls=%async_computation | async-start | bytes 524288 | tf_op jit(solution)/shard_map/all_to_all | solution.py:46
  60.9 0.0 all-reduce.3.cloned.1.call-start
  61.0 0.2 reshape.80
  61.1 2.5 convolution_convert_fusion.1
  63.6 14.1 %all-to-all-done = bf16[64,3,512]{2,1,0:T(4,128)(2,1)S(1)} async-done(((bf16[64,3,512]{2,1,0:T(4,128)(2,1)}), bf16[64,3,512]{2,1,0:T(4,128)(2,1)S(1)}, u32[]{:S(2)}, u32[]{:S(2)}) %all-to-all-start) | async-done | bytes 196640 | tf_op jit(solution)/shard_map/all_to_all | solution.py:46
  77.7 0.2 reshape.76
  77.9 0.0 copy-done
  77.9 1.5 convolution_convert_fusion
  79.4 0.0 all-reduce.3.cloned.1.call-update
  79.4 138.4 %all-reduce.3.cloned.1.call-done = (bf16[192,2048]{1,0:T(8,128)(2,1)}, bf16[192,1024]{1,0:T(8,128)(2,1)}) async-done(((bf16[192,2048]{1,0:T(8,128)(2,1)}, bf16[192,1024]{1,0:T(8,128)(2,1)}), (bf16[192,2048]{1,0:T(8,128)(2,1)}, bf16[192,1024]{1,0:T(8,128)(2,1)})) %all-reduce.3.cloned.1.call-update) | async-done | bytes 1179664 | tf_op jit(solution)/shard_map/psum | solution.py:62
  217.9 0.0 copy-start.6
  217.9 1.3 convert_element_type.65
  219.2 0.0 copy-start.1
  219.2 1.1 copy-done.1
  220.4 0.0 copy-done.6
  220.4 0.5 fusion.11
  220.9 0.0 copy-start.2
  220.9 0.8 fusion.5
  221.8 0.8 reshape.81
  222.6 17.9 %all-to-all-start.3 = ((bf16[64,3,512]{2,1,0:T(4,128)(2,1)}), bf16[64,3,512]{2,1,0:T(4,128)(2,1)S(1)}, u32[]{:S(2)}, u32[]{:S(2)}) async-start(bf16[64,3,512]{2,1,0:T(4,128)(2,1)} %reshape.81), calls=%async_computation.3 | async-start | bytes 524288 | tf_op jit(solution)/shard_map/all_to_all | solution.py:74
  240.5 0.0 copy-done.2
  240.5 2.4 convolution_convert_fusion.2
  242.9 1.7 reshape.77
  244.7 12.6 %all-to-all-done.3 = bf16[64,3,512]{2,1,0:T(4,128)(2,1)S(1)} async-done(((bf16[64,3,512]{2,1,0:T(4,128)(2,1)}), bf16[64,3,512]{2,1,0:T(4,128)(2,1)S(1)}, u32[]{:S(2)}, u32[]{:S(2)}) %all-to-all-start.3) | async-done | bytes 196640 | tf_op jit(solution)/shard_map/all_to_all | solution.py:74
  257.3 6.4 %all-to-all-start.1 = ((bf16[64,3,512]{2,1,0:T(4,128)(2,1)}), bf16[64,3,512]{2,1,0:T(4,128)(2,1)S(1)}, u32[]{:S(2)}, u32[]{:S(2)}) async-start(bf16[64,3,512]{2,1,0:T(4,128)(2,1)} %reshape.77), calls=%async_computation.1 | async-start | bytes 524288 | tf_op jit(solution)/shard_map/all_to_all | solution.py:71
  263.7 0.0 copy-start.3
  263.7 0.0 copy-start.5
  263.7 0.2 reshape.85
  263.9 1.2 convolution_reduce_fusion
  265.1 15.3 %all-to-all-done.1 = bf16[64,3,512]{2,1,0:T(4,128)(2,1)S(1)} async-done(((bf16[64,3,512]{2,1,0:T(4,128)(2,1)}), bf16[64,3,512]{2,1,0:T(4,128)(2,1)S(1)}, u32[]{:S(2)}, u32[]{:S(2)}) %all-to-all-start.1) | async-done | bytes 196640 | tf_op jit(solution)/shard_map/all_to_all | solution.py:71
  280.4 0.2 reshape.83
  280.6 0.4 fusion.3
  281.1 0.0 copy-done.3
  281.1 0.0 copy-done.5
  281.1 2.0 add_convert_fusion
  (5 shorter events, 0.1 us)
Async XLA Ops:
  7.2 70.7 %copy-start = (bf16[1,512,2048]{2,1,0:T(8,128)(2,1)S(1)}, bf16[1,512,2048]{2,1,0:T(8,128)(2,1)}, u32[]{:S(2)}) copy-start(bf16[1,512,2048]{2,1,0:T(8,128)(2,1)} %param.10) | copy-start | bytes 6291460
  7.2 4.8 %copy-start.7 = (s32[256,2]{0,1:T(2,128)S(1)}, s32[256,2]{0,1:T(2,128)}, u32[]{:S(2)}) copy-start(s32[256,2]{0,1:T(2,128)} %param.8) | copy-start | bytes 6148
  7.2 4.8 %copy-start.8 = (f32[256,2]{0,1:T(2,128)S(1)}, f32[256,2]{0,1:T(2,128)}, u32[]{:S(2)}) copy-start(f32[256,2]{0,1:T(2,128)} %param.9) | copy-start | bytes 6148
  10.0 26.6 %copy-start.4 = (bf16[256,512]{1,0:T(8,128)(2,1)S(1)}, bf16[256,512]{1,0:T(8,128)(2,1)}, u32[]{:S(2)}) copy-start(bf16[256,512]{1,0:T(8,128)(2,1)} %param.6) | copy-start | bytes 786436
  13.2 40.2 %all-to-all-start.2 = ((bf16[64,3,512]{2,1,0:T(4,128)(2,1)}), bf16[64,3,512]{2,1,0:T(4,128)(2,1)S(1)}, u32[]{:S(2)}, u32[]{:S(2)}) async-start(bf16[64,3,512]{2,1,0:T(4,128)(2,1)} %reshape.79), calls=%async_computation.2 | async-start | bytes 524288 | tf_op jit(solution)/shard_map/all_to_all | solution.py:49
  53.4 24.3 %all-to-all-start = ((bf16[64,3,512]{2,1,0:T(4,128)(2,1)}), bf16[64,3,512]{2,1,0:T(4,128)(2,1)S(1)}, u32[]{:S(2)}, u32[]{:S(2)}) async-start(bf16[64,3,512]{2,1,0:T(4,128)(2,1)} %reshape.75), calls=%async_computation | async-start | bytes 524288 | tf_op jit(solution)/shard_map/all_to_all | solution.py:46
  60.9 156.9 %all-reduce.3.cloned.1.call-start = ((), (), s32[]{:S(2)}) async-start(), calls=%async_computation.4 | async-start | bytes 2359296 | tf_op jit(solution)/shard_map/psum | solution.py:62
  217.9 2.5 copy-start.6
  219.2 1.2 copy-start.1
  220.9 19.6 %copy-start.2 = (bf16[1,1024,512]{2,1,0:T(8,128)(2,1)S(1)}, bf16[1,1024,512]{2,1,0:T(8,128)(2,1)}, u32[]{:S(2)}) copy-start(bf16[1,1024,512]{2,1,0:T(8,128)(2,1)} %param.11) | copy-start | bytes 3145732
  222.6 34.7 %all-to-all-start.3 = ((bf16[64,3,512]{2,1,0:T(4,128)(2,1)}), bf16[64,3,512]{2,1,0:T(4,128)(2,1)S(1)}, u32[]{:S(2)}, u32[]{:S(2)}) async-start(bf16[64,3,512]{2,1,0:T(4,128)(2,1)} %reshape.81), calls=%async_computation.3 | async-start | bytes 524288 | tf_op jit(solution)/shard_map/all_to_all | solution.py:74
  257.3 23.2 %all-to-all-start.1 = ((bf16[64,3,512]{2,1,0:T(4,128)(2,1)}), bf16[64,3,512]{2,1,0:T(4,128)(2,1)S(1)}, u32[]{:S(2)}, u32[]{:S(2)}) async-start(bf16[64,3,512]{2,1,0:T(4,128)(2,1)} %reshape.77), calls=%async_computation.1 | async-start | bytes 524288 | tf_op jit(solution)/shard_map/all_to_all | solution.py:71
  263.7 17.4 %copy-start.3 = (bf16[256,512]{1,0:T(8,128)(2,1)S(1)}, bf16[256,512]{1,0:T(8,128)(2,1)}, u32[]{:S(2)}) copy-start(bf16[256,512]{1,0:T(8,128)(2,1)} %param.7) | copy-start | bytes 786436
  263.7 17.4 %copy-start.5 = (bf16[256,512]{1,0:T(8,128)(2,1)S(1)}, bf16[256,512]{1,0:T(8,128)(2,1)}, u32[]{:S(2)}) copy-start(bf16[256,512]{1,0:T(8,128)(2,1)} %param.6) | copy-start | bytes 786436
Sparse Core Ops, SparseCore 0:
  79.5 138.2 all-reduce.2
where the time goes:
time: 291 us; the launch traced here: 290 us
  waiting for transfers between devices  196 us (67%)
  starting transfers between devices  55.1 us (19%)
  between operations  14.3 us (5%)
  matrix products  9.5 us (3%)
  local copies, waits for them, and re-layouts  7.76 us (3%)
  other arithmetic  7.11 us (2%)
    psum x1, waiting for transfers between devices, per_device(): lax.psum(gate_part_sum.astype(jnp.bfloat16), 'dp').astype(jnp.float32)  138 us
    all_to_all x1, starting transfers between devices, per_device(): lax.all_to_all(send_grads.reshape(n_dev, CAP, width), 'expert', split_axi...  23.2 us
    all_to_all x1, starting transfers between devices, per_device(): lax.all_to_all(row_grad.reshape(n_dev, CAP, width), 'expert', split_axis=...  17.9 us
    all_to_all x1, waiting for transfers between devices, per_device(): lax.all_to_all(send_grads.reshape(n_dev, CAP, width), 'expert', split_axi...  15.7 us
    all_to_all x1, waiting for transfers between devices, per_device(): lax.all_to_all(expert_out.reshape(n_dev, CAP, width), 'expert', split_axi...  15.3 us
    all_to_all x1, waiting for transfers between devices, per_device(): lax.all_to_all(send_rows.reshape(n_dev, CAP, width), 'expert', split_axis...  14.1 us
    all_to_all x1, waiting for transfers between devices, per_device(): lax.all_to_all(row_grad.reshape(n_dev, CAP, width), 'expert', split_axis=...  12.6 us
    all_to_all x1, starting transfers between devices, per_device(): lax.all_to_all(send_rows.reshape(n_dev, CAP, width), 'expert', split_axis...  7.5 us
  transfers between devices with their start and end apart: 5, of which 5 were waited for; matrix products, arithmetic and copies ran while one was open for 3% of the time, Pallas kernels for 0%

commit v1 on v0

v1 whole, which is shorter than its diff:
```python
import functools

import jax
import jax.numpy as jnp
from jax import lax
from jax.experimental import pallas as pl
from jax.experimental.pallas import tpu as pltpu
from jax.sharding import PartitionSpec as P

CAP = 3
LANES = 128
BF = jnp.bfloat16
F32 = jnp.float32
VMEM = pl.BlockSpec(memory_space=pltpu.VMEM)
SMEM = pl.BlockSpec(memory_space=pltpu.SMEM)


def call(body, outs, operands, scratch=(), flops=0):
    size = sum(o.size * o.dtype.itemsize for o in outs)
    size += sum(o.size * o.dtype.itemsize for o in operands)
    return pl.pallas_call(
        body,
        out_shape=list(outs),
        in_specs=[SMEM if o.ndim == 1 else VMEM for o in operands],
        out_specs=[VMEM] * len(outs),
        scratch_shapes=list(scratch),
        compiler_params=pltpu.CompilerParams(vmem_limit_bytes=32 * 1024 * 1024),
        cost_estimate=pl.CostEstimate(flops=flops, bytes_accessed=size, transcendentals=0),
    )(*operands)


def dot(a, b):
    return jnp.dot(a, b, preferred_element_type=F32)


def dot_t(a, b):
    return lax.dot_general(a, b, (((1,), (1,)), ((), ())), preferred_element_type=F32)


def pack(values, wide, n_dev):
    pieces = values[0].shape[1] // LANES
    stride = 2 * CAP * pieces
    for a, value in enumerate(values):
        for j in range(CAP):
            for q in range(pieces):
                place = (a * CAP + j) * pieces + q
                wide[pl.ds(place, n_dev, stride=stride), :] = value[
                    j * n_dev : (j + 1) * n_dev, q * LANES : (q + 1) * LANES
                ]


def unpack(wide, a, n_dev, width):
    pieces = width // LANES
    stride = 2 * CAP * pieces
    rows = []
    for j in range(CAP):
        columns = [
            wide[pl.ds((a * CAP + j) * pieces + q, n_dev, stride=stride), :] for q in range(pieces)
        ]
        rows.append(jnp.concatenate(columns, axis=1))
    return jnp.concatenate(rows, axis=0)


def send_body(n_dev, ids, gates, tokens, grad_out, send, picks, wide):
    t = tokens.shape[0]
    expert = lax.broadcasted_iota(jnp.int32, (n_dev, t), 0)
    hot = [jnp.where(expert == ids[k : k + 1, :], 1.0, 0.0) for k in range(2)]
    earlier = lax.broadcasted_iota(jnp.int32, (t, t), 0) < lax.broadcasted_iota(jnp.int32, (t, t), 1)
    before = dot((hot[0] + hot[1]).astype(BF), jnp.where(earlier, 1.0, 0.0).astype(BF))
    before = [before, before + hot[0]]
    picked = [
        jnp.concatenate(
            [jnp.where(before[k] == float(j), hot[k], 0.0) for j in range(CAP)], axis=0
        )
        for k in range(2)
    ]
    gate = jnp.sum(picked[0] * gates[0:1, :] + picked[1] * gates[1:2, :], axis=1, keepdims=True)
    both = (picked[0] + picked[1]).astype(BF)
    pack([dot(both, tokens[...]), dot(both, grad_out[...]) * gate], wide, n_dev)
    send[...] = wide[...].astype(BF)
    picks[...] = jnp.concatenate(picked, axis=1).astype(BF)


def first_body(n_dev, core, recv, w_in, w_out, partial, kept, wide, rows_x, rows_g):
    wide[...] = recv[...].astype(F32)
    width = w_in.shape[0]
    rows_x[...] = unpack(wide, 0, n_dev, width).astype(BF)
    rows_g[...] = unpack(wide, 1, n_dev, width).astype(BF)
    count = partial.shape[0]
    other = pl.ds(pl.multiple_of((1 - core[0]) * count, count), count)
    own = pl.ds(pl.multiple_of(core[0] * count, count), count)
    kept[:, :width] = rows_x[own, :]
    kept[:, width:] = rows_g[own, :]
    partial[:, : w_in.shape[1]] = dot(rows_x[other, :], w_in[...]).astype(BF)
    partial[:, w_in.shape[1] :] = dot_t(rows_g[other, :], w_out[...]).astype(BF)


def second_body(kept, w_in, w_out, partial):
    width = w_in.shape[0]
    partial[:, : w_in.shape[1]] = dot(kept[:, :width], w_in[...]).astype(BF)
    partial[:, w_in.shape[1] :] = dot_t(kept[:, width:], w_out[...]).astype(BF)


def own_body(hidden, w_in, w_out, rows):
    half, width = w_out.shape
    rows[:, :width] = dot(hidden[:, :half], w_out[...]).astype(BF)
    rows[:, width:] = dot_t(hidden[:, half:], w_in[...]).astype(BF)


def back_body(n_dev, core, hidden, own_rows, w_in, w_out, send, wide, rows):
    half, width = w_out.shape
    count = hidden.shape[0]
    other = pl.ds(pl.multiple_of((1 - core[0]) * count, count), count)
    own = pl.ds(pl.multiple_of(core[0] * count, count), count)
    rows[own, :] = own_rows[...].astype(F32)
    rows[other, :width] = dot(hidden[:, :half], w_out[...])
    rows[other, width:] = dot_t(hidden[:, half:], w_in[...])
    pack([rows[:, :width], rows[:, width:]], wide, n_dev)
    send[...] = wide[...].astype(BF)


def combine_body(n_dev, recv, picks, ids, gates, tokens, grad_out, moe_out, grad_tokens, wide):
    t, width = tokens.shape
    wide[...] = recv[...].astype(F32)
    back_out = unpack(wide, 0, n_dev, width).astype(BF)
    back_grad = unpack(wide, 1, n_dev, width).astype(BF)
    take = [picks[:, k * t : (k + 1) * t].astype(F32).T.astype(BF) for k in range(2)]
    copied = jnp.sum(jnp.where(ids[...] >= n_dev, gates[...], 0.0), axis=1, keepdims=True)
    moe = gates[:, 0:1] * dot(take[0], back_out) + gates[:, 1:2] * dot(take[1], back_out)
    moe_out[...] = (moe + copied * tokens[...].astype(F32)).astype(BF)
    grad = dot(take[0] + take[1], back_grad)
    grad_tokens[...] = (grad + copied * grad_out[...].astype(F32)).astype(BF)


def slice_of(array, start, count):
    return lax.dynamic_slice_in_dim(array, start, count, axis=0)


def per_device(tokens, grad_out, expert_ids, gates, w_in, w_out):
    n_dev = lax.axis_size("expert")
    n_dp = lax.axis_size("dp")
    t, width = tokens.shape
    half = w_out.shape[1]
    count = n_dev * CAP
    wide_rows = 2 * count * width // LANES
    w_first, w_second = w_in[0], w_out[0]
    wide = pltpu.VMEM((wide_rows, LANES), F32)
    shape = jax.ShapeDtypeStruct

    me = lax.axis_index("dp")
    core, pair, third = me % 2, (me // 2) % 2, me // 4
    cores = [(i, i ^ 1) for i in range(n_dp)]
    pairs = [(i, i ^ 2) for i in range(n_dp)]
    next_third = [(i, (i + 4) % n_dp) for i in range(n_dp)]
    last_third = [(i, (i + 8) % n_dp) for i in range(n_dp)]
    core_ref = core.astype(jnp.int32).reshape(1)

    send, picks = call(
        functools.partial(send_body, n_dev),
        [shape((wide_rows, LANES), BF), shape((count, 2 * t), BF)],
        [expert_ids.T, gates.T, tokens, grad_out],
        [wide],
        2 * (2 * count * t * width + n_dev * t * t),
    )

    def exchange(rows):
        parts = rows.reshape(n_dev, wide_rows // n_dev, LANES)
        parts = lax.all_to_all(parts, "expert", split_axis=0, concat_axis=0, tiled=True)
        return parts.reshape(wide_rows, LANES)

    recv = exchange(send)

    hidden_width = 3 * half
    n_core, n_pair, n_third = count // 2, count // 4, count // 12
    flops = 2 * n_core * width * hidden_width
    to_core, kept_rows = call(
        functools.partial(first_body, n_dev),
        [shape((n_core, hidden_width), BF), shape((n_core, 2 * width), BF)],
        [core_ref, recv, w_first, w_second],
        [wide, pltpu.VMEM((count, width), BF), pltpu.VMEM((count, width), BF)],
        flops,
    )
    from_core = lax.ppermute(to_core, "dp", cores)
    (mine,) = call(
        second_body, [shape((n_core, hidden_width), BF)], [kept_rows, w_first, w_second], [], flops
    )

    def two(start, rows):
        return slice_of(mine, start, rows).astype(F32) + slice_of(from_core, start, rows).astype(F32)

    from_pair = lax.ppermute(two((1 - pair) * n_pair, n_pair).astype(BF), "dp", pairs)

    def four(block):
        start = block * n_third
        return two(pair * n_pair + start, n_third) + slice_of(from_pair, start, n_third).astype(F32)

    after, before = (third + 1) % 3, (third + 2) % 3
    from_before = lax.ppermute(four(after).astype(BF), "dp", next_third)
    from_after = lax.ppermute(four(before).astype(BF), "dp", last_third)
    total = four(third) + from_before.astype(F32) + from_after.astype(F32)

    gate_part, up_part, hidden_grad = total[:, :half], total[:, half : 2 * half], total[:, 2 * half :]
    sig = jax.nn.sigmoid(gate_part)
    silu = gate_part * sig
    dsilu = sig * (1.0 + gate_part * (1.0 - sig))
    block = jnp.concatenate(
        [silu * up_part, hidden_grad * up_part * dsilu, hidden_grad * silu], axis=1
    ).astype(BF)

    of_before = lax.ppermute(block, "dp", next_third)
    of_after = lax.ppermute(block, "dp", last_third)
    ring = jnp.concatenate([block, of_after, of_before, block, of_after], axis=0)
    quarter = slice_of(ring, ((3 - third) % 3) * n_third, n_pair)
    other_quarter = lax.ppermute(quarter, "dp", pairs)
    own_half = jnp.concatenate(
        [
            jnp.where(pair == 0, quarter, other_quarter),
            jnp.where(pair == 0, other_quarter, quarter),
        ],
        axis=0,
    )
    other_half = lax.ppermute(own_half, "dp", cores)
    (own_rows,) = call(
        own_body, [shape((n_core, 2 * width), BF)], [own_half, w_first, w_second], [], flops
    )
    (send_back,) = call(
        functools.partial(back_body, n_dev),
        [shape((wide_rows, LANES), BF)],
        [core_ref, other_half, own_rows, w_first, w_second],
        [wide, pltpu.VMEM((count, 2 * width), F32)],
        flops,
    )
    recv_back = exchange(send_back)

    moe_out, grad_tokens = call(
        functools.partial(combine_body, n_dev),
        [shape((t, width), BF), shape((t, width), BF)],
        [recv_back, picks, expert_ids, gates, tokens, grad_out],
        [wide],
        2 * 3 * count * t * width,
    )
    return moe_out, grad_tokens


def solution(mesh):
    in_specs = (
        P("expert", "dp"),
        P("expert", "dp"),
        P("expert", None),
        P("expert", None),
        P("expert", "dp", None),
        P("expert", None, "dp"),
    )
    out_specs = (P("expert", "dp"), P("expert", "dp"))
    return jax.shard_map(
        per_device, mesh=mesh, in_specs=in_specs, out_specs=out_specs, check_vma=False
    )
```

time: 291 us -> 165 us (0.57)
  the two profiles are of different devices: /device:TPU:8 before, /device:TPU:64 now
where the time goes in v1:
time: 165 us; the launch traced here: 164 us
  waiting for transfers between devices  84.8 us (51%)
  starting transfers between devices  54.4 us (33%)
  local copies, waits for them, and re-layouts  10.1 us (6%)
  Pallas kernels  7.84 us (5%)
  other arithmetic  5.81 us (4%)
    all_to_all x2, waiting for transfers between devices, exchange(): lax.all_to_all(parts, 'expert', split_axis=0, concat_axis=0, tiled=True)  54.6 us
    all_to_all x2, starting transfers between devices, exchange(): lax.all_to_all(parts, 'expert', split_axis=0, concat_axis=0, tiled=True)  27.1 us
    ppermute x1, waiting for transfers between devices, per_device(): lax.ppermute(two((1 - pair) * n_pair, n_pair).astype(BF), 'dp', pairs)  9.41 us
    unnamed x36, local copies, waits for them, and re-layouts  8.42 us
    ppermute x1, starting transfers between devices, per_device(): of_after = lax.ppermute(block, 'dp', last_third)  7.94 us
    pallas_call x6, Pallas kernels, call(): pl.pallas_call(body, out_shape=list(outs), in_specs=[SMEM if o.ndim == 1...  7.84 us
    ppermute x1, starting transfers between devices, per_device(): from_after = lax.ppermute(four(before).astype(BF), 'dp', last_third)  7.47 us
    ppermute x1, waiting for transfers between devices, per_device(): other_quarter = lax.ppermute(quarter, 'dp', pairs)  7.39 us
  transfers between devices with their start and end apart: 10, of which 10 were waited for; matrix products, arithmetic and copies ran while one was open for 1% of the time, Pallas kernels for 1%

profile of v1, /device:TPU:64, one launch (start us, length us, event | category | flops | bytes accessed | tf_op | source)
XLA Modules:
  0.0 163.9 jit_solution(14729359887146286387)
XLA Ops:
  0.6 0.0 copy-start.2
  0.6 0.0 copy-start.4
  0.7 1.0 copy-done.4
  1.7 0.0 copy-start.6
  1.7 0.9 copy-done.6
  2.6 0.0 copy-start.12
  2.6 0.7 copy-done.12
  3.3 0.0 copy-start.14
  3.3 0.7 copy-done.14
  4.0 1.2 shard_map.77
  5.2 22.3 %all-to-all-start = ((bf16[64,24,128]{2,1,0:T(8,128)(2,1)}), bf16[64,24,128]{2,1,0:T(8,128)(2,1)S(1)}, u32[]{:S(2)}, u32[]{:S(2)}) async-start(bf16[64,24,128]{2,1,0:T(8,128)(2,1)} %bitcast.3), calls=%async_computation | async-start | bytes 786432 | tf_op jit(solution)/shard_map/all_to_all | solution.py:168
  27.6 26.9 %all-to-all-done = bf16[64,24,128]{2,1,0:T(8,128)(2,1)S(1)} async-done(((bf16[64,24,128]{2,1,0:T(8,128)(2,1)}), bf16[64,24,128]{2,1,0:T(8,128)(2,1)S(1)}, u32[]{:S(2)}, u32[]{:S(2)}) %all-to-all-start) | async-done | bytes 393248 | tf_op jit(solution)/shard_map/all_to_all | solution.py:168
  54.5 0.0 copy-done.8
  54.5 0.0 copy-done.2
  54.5 1.6 copy-done
  56.1 1.7 %shard_map.78 = (bf16[96,3072]{1,0:T(8,128)(2,1)}, bf16[96,1024]{1,0:T(8,128)(2,1)S(1)}) custom-call(s32[1]{0:T(128)} %bitcast.core, bf16[1536,128]{1,0:T(8,128)(2,1)S(1)} %bitcast.18, bf16[512,2048]{1,0:T(8,128)(2,1)S(1)} %bitcast.9, bf16[1024,512]{1,0:T(8,128)(2,1)S(1)} %bitcast.13), custom_call_target="tpu_custom_call" | custom-call | flops 301989888 | bytes 4325380 | tf_op jit(solution)/shard_map/pallas_call | solution.py:21
  57.9 0.7 copy-done.10
  58.5 1.9 %collective-permute-start = (bf16[96,3072]{1,0:T(8,128)(2,1)}, bf16[96,3072]{1,0:T(8,128)(2,1)}, u32[]{:S(2)}, u32[]{:S(2)}) collective-permute-start(bf16[96,3072]{1,0:T(8,128)(2,1)} %get-tuple-element.8), channel_id=1, source_target_pairs={{0,64},{64,0},{128,192},{192,128},{256,320},{320,256},{384,448},{4... | collective-permute-start | bytes 1769480 | tf_op jit(solution)/shard_map/ppermute | solution.py:183
  60.5 0.0 copy-done.1
  60.5 0.0 copy-start.11
  60.5 0.9 copy-done.11
  61.4 0.8 shard_map.79
  62.2 0.0 copy-start.3
  62.2 0.5 collective-permute-done
  62.8 0.3 copy-done.3
  63.1 1.0 add_convert_fusion
  64.1 1.9 %collective-permute-start.1 = (bf16[48,3072]{1,0:T(8,128)(2,1)S(1)}, bf16[48,3072]{1,0:T(8,128)(2,1)}, u32[]{:S(2)}, u32[]{:S(2)}) collective-permute-start(bf16[48,3072]{1,0:T(8,128)(2,1)S(1)} %add_convert_fusion), channel_id=1, source_target_pairs={{0,128},{64,192},{128,0},{192,64},{256,384},{320,448},{384,256},{4... | collective-permute-start | bytes 884744 | tf_op jit(solution)/shard_map/ppermute | solution.py:191
  66.1 9.4 %collective-permute-done.1 = bf16[48,3072]{1,0:T(8,128)(2,1)} collective-permute-done((bf16[48,3072]{1,0:T(8,128)(2,1)S(1)}, bf16[48,3072]{1,0:T(8,128)(2,1)}, u32[]{:S(2)}, u32[]{:S(2)}) %collective-permute-start.1) | collective-permute-done | bytes 294944 | tf_op jit(solution)/shard_map/ppermute | solution.py:191
  75.5 1.2 add_convert_fusion.2
  76.7 2.3 %collective-permute-start.2 = (bf16[16,3072]{1,0:T(8,128)(2,1)S(1)}, bf16[16,3072]{1,0:T(8,128)(2,1)S(1)}, u32[]{:S(2)}, u32[]{:S(2)}) collective-permute-start(bf16[16,3072]{1,0:T(8,128)(2,1)S(1)} %get-tuple-element.10), channel_id=1, source_target_pairs={{0,256},{64,320},{128,384},{192,448},{256,512},{320,576},{384,640}... | collective-permute-start | bytes 294920 | tf_op jit(solution)/shard_map/ppermute | solution.py:198
  79.0 7.5 %collective-permute-start.3 = (bf16[16,3072]{1,0:T(8,128)(2,1)S(1)}, bf16[16,3072]{1,0:T(8,128)(2,1)S(1)}, u32[]{:S(2)}, u32[]{:S(2)}) collective-permute-start(bf16[16,3072]{1,0:T(8,128)(2,1)S(1)} %get-tuple-element.11), channel_id=1, source_target_pairs={{0,512},{64,576},{128,640},{192,704},{256,0},{320,64},{384,128},{4... | collective-permute-start | bytes 294920 | tf_op jit(solution)/shard_map/ppermute | solution.py:199
  86.5 0.8 collective-permute-done.2
  87.3 3.2 %collective-permute-done.3 = bf16[16,3072]{1,0:T(8,128)(2,1)S(1)} collective-permute-done((bf16[16,3072]{1,0:T(8,128)(2,1)S(1)}, bf16[16,3072]{1,0:T(8,128)(2,1)S(1)}, u32[]{:S(2)}, u32[]{:S(2)}) %collective-permute-start.3) | collective-permute-done | bytes 98336 | tf_op jit(solution)/shard_map/ppermute | solution.py:199
  90.5 1.0 convert_add_fusion
  91.6 0.1 multiply_convert_fusion.2
  91.6 0.6 pad_maximum_fusion.1
  92.3 7.9 %collective-permute-start.4 = (bf16[16,3072]{1,0:T(8,128)(2,1)S(1)}, bf16[16,3072]{1,0:T(8,128)(2,1)S(1)}, u32[]{:S(2)}, u32[]{:S(2)}) collective-permute-start(bf16[16,3072]{1,0:T(8,128)(2,1)S(1)} %get-tuple-element.17), channel_id=1, source_target_pairs={{0,512},{64,576},{128,640},{192,704},{256,0},{320,64},{384,128},{4... | collective-permute-start | bytes 294920 | tf_op jit(solution)/shard_map/ppermute | solution.py:211
  100.2 1.9 %collective-permute-start.5 = (bf16[16,3072]{1,0:T(8,128)(2,1)S(1)}, bf16[16,3072]{1,0:T(8,128)(2,1)S(1)}, u32[]{:S(2)}, u32[]{:S(2)}) collective-permute-start(bf16[16,3072]{1,0:T(8,128)(2,1)S(1)} %get-tuple-element.17), channel_id=1, source_target_pairs={{0,256},{64,320},{128,384},{192,448},{256,512},{320,576},{384,640}... | collective-permute-start | bytes 294920 | tf_op jit(solution)/shard_map/ppermute | solution.py:210
  102.2 3.3 %collective-permute-done.4 = bf16[16,3072]{1,0:T(8,128)(2,1)S(1)} collective-permute-done((bf16[16,3072]{1,0:T(8,128)(2,1)S(1)}, bf16[16,3072]{1,0:T(8,128)(2,1)S(1)}, u32[]{:S(2)}, u32[]{:S(2)}) %collective-permute-start.4) | collective-permute-done | bytes 98336 | tf_op jit(solution)/shard_map/ppermute | solution.py:211
  105.5 0.6 constant_dynamic-update-slice_fusion.3
  106.1 4.5 %collective-permute-done.5 = bf16[16,3072]{1,0:T(8,128)(2,1)S(1)} collective-permute-done((bf16[16,3072]{1,0:T(8,128)(2,1)S(1)}, bf16[16,3072]{1,0:T(8,128)(2,1)S(1)}, u32[]{:S(2)}, u32[]{:S(2)}) %collective-permute-start.5) | collective-permute-done | bytes 98336 | tf_op jit(solution)/shard_map/ppermute | solution.py:210
  110.6 0.6 constant_dynamic-update-slice_fusion.2
  111.3 0.6 constant_dynamic-update-slice_fusion.1
  111.9 0.7 constant_dynamic-update-slice_fusion
  112.6 1.0 constant_dynamic-slice_fusion
  113.6 1.9 %collective-permute-start.6 = (bf16[48,3072]{1,0:T(8,128)(2,1)S(1)}, bf16[48,3072]{1,0:T(8,128)(2,1)}, u32[]{:S(2)}, u32[]{:S(2)}) collective-permute-start(bf16[48,3072]{1,0:T(8,128)(2,1)S(1)} %constant_dynamic-slice_fusion), channel_id=1, source_target_pairs={{0,128},{64,192},{128,0},{192,64},{256,384},{320,448},{384,256},{4... | collective-permute-start | bytes 884744 | tf_op jit(solution)/shard_map/ppermute | solution.py:214
  115.5 7.4 %collective-permute-done.6 = bf16[48,3072]{1,0:T(8,128)(2,1)} collective-permute-done((bf16[48,3072]{1,0:T(8,128)(2,1)S(1)}, bf16[48,3072]{1,0:T(8,128)(2,1)}, u32[]{:S(2)}, u32[]{:S(2)}) %collective-permute-start.6) | collective-permute-done | bytes 294944 | tf_op jit(solution)/shard_map/ppermute | solution.py:214
  122.9 1.1 broadcast_select_fusion.1
  124.1 1.9 %collective-permute-start.7 = (bf16[96,3072]{1,0:T(8,128)(2,1)S(1)}, bf16[96,3072]{1,0:T(8,128)(2,1)S(1)}, u32[]{:S(2)}, u32[]{:S(2)}) collective-permute-start(bf16[96,3072]{1,0:T(8,128)(2,1)S(1)} %pad_maximum_fusion.hidden), channel_id=1, source_target_pairs={{0,64},{64,0},{128,192},{192,128},{256,320},{320,256},{384,448},{4... | collective-permute-start | bytes 1769480 | tf_op jit(solution)/shard_map/ppermute | solution.py:222
  126.0 0.9 shard_map.80.own_rows
  127.0 0.0 copy-start.13
  127.0 0.0 copy-start.15
  127.0 1.0 collective-permute-done.7.hidden
  128.0 1.8 %shard_map.81 = bf16[1536,128]{1,0:T(8,128)(2,1)} custom-call(s32[1]{0:T(128)} %bitcast.core, bf16[96,3072]{1,0:T(8,128)(2,1)S(1)} %collective-permute-done.7.hidden, bf16[96,1024]{1,0:T(8,128)(2,1)S(1)} %shard_map.80.own_rows, bf16[512,2048]{1,0:T(8,128)(2,1)S(1)} %bitcast.12, bf16[1024,512]{1,0:T(8,128)(2,1)S(1)} %bitcast.16), custom_call_target="tpu_custom_call" | custom-call | flops 301989888 | bytes 4325380 | tf_op jit(solution)/shard_map/pallas_call | solution.py:21
  129.8 4.8 %all-to-all-start.1 = ((bf16[64,24,128]{2,1,0:T(8,128)(2,1)}), bf16[64,24,128]{2,1,0:T(8,128)(2,1)S(1)}, u32[]{:S(2)}, u32[]{:S(2)}) async-start(bf16[64,24,128]{2,1,0:T(8,128)(2,1)} %bitcast.7), calls=%async_computation.1 | async-start | bytes 786432 | tf_op jit(solution)/shard_map/all_to_all | solution.py:168
  134.6 0.0 copy-done.13
  134.6 0.1 copy.8.ids
  134.8 0.0 copy-done.15
  134.8 0.1 copy.9.gates
  134.9 27.6 %all-to-all-done.1 = bf16[64,24,128]{2,1,0:T(8,128)(2,1)S(1)} async-done(((bf16[64,24,128]{2,1,0:T(8,128)(2,1)}), bf16[64,24,128]{2,1,0:T(8,128)(2,1)S(1)}, u32[]{:S(2)}, u32[]{:S(2)}) %all-to-all-start.1) | async-done | bytes 393248 | tf_op jit(solution)/shard_map/all_to_all | solution.py:168
  162.5 0.0 copy-done.5
  162.5 0.0 copy-done.7
  162.5 0.0 copy-done.9
  162.5 1.3 shard_map.82
  (8 shorter events, 0.1 us)
Async XLA Ops:
  0.6 53.9 %copy-start.2 = (bf16[1,1024,512]{2,1,0:T(8,128)(2,1)S(1)}, bf16[1,1024,512]{2,1,0:T(8,128)(2,1)}, u32[]{:S(2)}) copy-start(bf16[1,1024,512]{2,1,0:T(8,128)(2,1)} %param.11) | copy-start | bytes 3145732
  0.6 1.0 copy-start.4
  1.7 0.9 copy-start.6
  2.6 0.7 copy-start.12
  3.3 0.7 copy-start.14
  5.2 49.3 %copy-start.8 = (bf16[192,512]{1,0:T(8,128)(2,1)}, bf16[192,512]{1,0:T(8,128)(2,1)S(1)}, u32[]{:S(2)}) copy-start(bf16[192,512]{1,0:T(8,128)(2,1)S(1)} %get-tuple-element.9.picks) | copy-start | bytes 589828
  5.2 49.3 %all-to-all-start = ((bf16[64,24,128]{2,1,0:T(8,128)(2,1)}), bf16[64,24,128]{2,1,0:T(8,128)(2,1)S(1)}, u32[]{:S(2)}, u32[]{:S(2)}) async-start(bf16[64,24,128]{2,1,0:T(8,128)(2,1)} %bitcast.3), calls=%async_computation | async-start | bytes 786432 | tf_op jit(solution)/shard_map/all_to_all | solution.py:168
  54.5 1.6 copy-start
  56.1 4.4 %copy-start.1 = (bf16[1,512,2048]{2,1,0:T(8,128)(2,1)S(1)}, bf16[1,512,2048]{2,1,0:T(8,128)(2,1)}, u32[]{:S(2)}) copy-start(bf16[1,512,2048]{2,1,0:T(8,128)(2,1)} %param.10) | copy-start | bytes 6291460
  57.9 0.7 copy-start.10
  58.5 4.2 %collective-permute-start = (bf16[96,3072]{1,0:T(8,128)(2,1)}, bf16[96,3072]{1,0:T(8,128)(2,1)}, u32[]{:S(2)}, u32[]{:S(2)}) collective-permute-start(bf16[96,3072]{1,0:T(8,128)(2,1)} %get-tuple-element.8), channel_id=1, source_target_pairs={{0,64},{64,0},{128,192},{192,128},{256,320},{320,256},{384,448},{4... | collective-permute-start | bytes 1769480 | tf_op jit(solution)/shard_map/ppermute | solution.py:183
  60.5 0.9 copy-start.11
  62.2 0.8 copy-start.3
  64.1 11.4 %collective-permute-start.1 = (bf16[48,3072]{1,0:T(8,128)(2,1)S(1)}, bf16[48,3072]{1,0:T(8,128)(2,1)}, u32[]{:S(2)}, u32[]{:S(2)}) collective-permute-start(bf16[48,3072]{1,0:T(8,128)(2,1)S(1)} %add_convert_fusion), channel_id=1, source_target_pairs={{0,128},{64,192},{128,0},{192,64},{256,384},{320,448},{384,256},{4... | collective-permute-start | bytes 884744 | tf_op jit(solution)/shard_map/ppermute | solution.py:191
  76.7 10.6 %collective-permute-start.2 = (bf16[16,3072]{1,0:T(8,128)(2,1)S(1)}, bf16[16,3072]{1,0:T(8,128)(2,1)S(1)}, u32[]{:S(2)}, u32[]{:S(2)}) collective-permute-start(bf16[16,3072]{1,0:T(8,128)(2,1)S(1)} %get-tuple-element.10), channel_id=1, source_target_pairs={{0,256},{64,320},{128,384},{192,448},{256,512},{320,576},{384,640}... | collective-permute-start | bytes 294920 | tf_op jit(solution)/shard_map/ppermute | solution.py:198
  79.0 11.5 %collective-permute-start.3 = (bf16[16,3072]{1,0:T(8,128)(2,1)S(1)}, bf16[16,3072]{1,0:T(8,128)(2,1)S(1)}, u32[]{:S(2)}, u32[]{:S(2)}) collective-permute-start(bf16[16,3072]{1,0:T(8,128)(2,1)S(1)} %get-tuple-element.11), channel_id=1, source_target_pairs={{0,512},{64,576},{128,640},{192,704},{256,0},{320,64},{384,128},{4... | collective-permute-start | bytes 294920 | tf_op jit(solution)/shard_map/ppermute | solution.py:199
  92.3 13.2 %collective-permute-start.4 = (bf16[16,3072]{1,0:T(8,128)(2,1)S(1)}, bf16[16,3072]{1,0:T(8,128)(2,1)S(1)}, u32[]{:S(2)}, u32[]{:S(2)}) collective-permute-start(bf16[16,3072]{1,0:T(8,128)(2,1)S(1)} %get-tuple-element.17), channel_id=1, source_target_pairs={{0,512},{64,576},{128,640},{192,704},{256,0},{320,64},{384,128},{4... | collective-permute-start | bytes 294920 | tf_op jit(solution)/shard_map/ppermute | solution.py:211
  100.2 10.4 %collective-permute-start.5 = (bf16[16,3072]{1,0:T(8,128)(2,1)S(1)}, bf16[16,3072]{1,0:T(8,128)(2,1)S(1)}, u32[]{:S(2)}, u32[]{:S(2)}) collective-permute-start(bf16[16,3072]{1,0:T(8,128)(2,1)S(1)} %get-tuple-element.17), channel_id=1, source_target_pairs={{0,256},{64,320},{128,384},{192,448},{256,512},{320,576},{384,640}... | collective-permute-start | bytes 294920 | tf_op jit(solution)/shard_map/ppermute | solution.py:210
  113.6 9.3 %collective-permute-start.6 = (bf16[48,3072]{1,0:T(8,128)(2,1)S(1)}, bf16[48,3072]{1,0:T(8,128)(2,1)}, u32[]{:S(2)}, u32[]{:S(2)}) collective-permute-start(bf16[48,3072]{1,0:T(8,128)(2,1)S(1)} %constant_dynamic-slice_fusion), channel_id=1, source_target_pairs={{0,128},{64,192},{128,0},{192,64},{256,384},{320,448},{384,256},{4... | collective-permute-start | bytes 884744 | tf_op jit(solution)/shard_map/ppermute | solution.py:214
  124.1 3.9 %collective-permute-start.7 = (bf16[96,3072]{1,0:T(8,128)(2,1)S(1)}, bf16[96,3072]{1,0:T(8,128)(2,1)S(1)}, u32[]{:S(2)}, u32[]{:S(2)}) collective-permute-start(bf16[96,3072]{1,0:T(8,128)(2,1)S(1)} %pad_maximum_fusion.hidden), channel_id=1, source_target_pairs={{0,64},{64,0},{128,192},{192,128},{256,320},{320,256},{384,448},{4... | collective-permute-start | bytes 1769480 | tf_op jit(solution)/shard_map/ppermute | solution.py:222
  127.0 7.6 %copy-start.13 = (s32[256,2]{0,1:T(2,128)S(1)}, s32[256,2]{0,1:T(2,128)}, u32[]{:S(2)}) copy-start(s32[256,2]{0,1:T(2,128)} %param.8) | copy-start | bytes 6148
  127.0 7.8 %copy-start.15 = (f32[256,2]{0,1:T(2,128)S(1)}, f32[256,2]{0,1:T(2,128)}, u32[]{:S(2)}) copy-start(f32[256,2]{0,1:T(2,128)} %param.9) | copy-start | bytes 6148
  129.8 32.7 %copy-start.5 = (bf16[256,512]{1,0:T(8,128)(2,1)S(1)}, bf16[256,512]{1,0:T(8,128)(2,1)}, u32[]{:S(2)}) copy-start(bf16[256,512]{1,0:T(8,128)(2,1)} %tokens.3) | copy-start | bytes 786436
  129.8 32.7 %copy-start.7 = (bf16[256,512]{1,0:T(8,128)(2,1)S(1)}, bf16[256,512]{1,0:T(8,128)(2,1)}, u32[]{:S(2)}) copy-start(bf16[256,512]{1,0:T(8,128)(2,1)} %grad_out.3) | copy-start | bytes 786436
  129.8 32.7 %copy-start.9 = (bf16[192,512]{1,0:T(8,128)(2,1)S(1)}, bf16[192,512]{1,0:T(8,128)(2,1)}, u32[]{:S(2)}) copy-start(bf16[192,512]{1,0:T(8,128)(2,1)} %copy-done.8) | copy-start | bytes 589828
  129.8 32.7 %all-to-all-start.1 = ((bf16[64,24,128]{2,1,0:T(8,128)(2,1)}), bf16[64,24,128]{2,1,0:T(8,128)(2,1)S(1)}, u32[]{:S(2)}, u32[]{:S(2)}) async-start(bf16[64,24,128]{2,1,0:T(8,128)(2,1)} %bitcast.7), calls=%async_computation.1 | async-start | bytes 786432 | tf_op jit(solution)/shard_map/all_to_all | solution.py:168

commit v2 on v1

v2 whole, which is shorter than its diff:
```python
import functools

import jax
import jax.numpy as jnp
from jax import lax
from jax.experimental import pallas as pl
from jax.experimental.pallas import tpu as pltpu
from jax.sharding import PartitionSpec as P

CAP = 3
LANES = 128
CHUNKS = 1
BF = jnp.bfloat16
F32 = jnp.float32
VMEM = pl.BlockSpec(memory_space=pltpu.VMEM)
SMEM = pl.BlockSpec(memory_space=pltpu.SMEM)
HBM = pl.BlockSpec(memory_space=pltpu.HBM)


def call(body, outs, operands, scratch=(), flops=0, far=()):
    operands = [
        pltpu.with_memory_space_constraint(o, pltpu.HBM) if i in far else o
        for i, o in enumerate(operands)
    ]
    size = sum(o.size * o.dtype.itemsize for o in outs)
    size += sum(o.size * o.dtype.itemsize for o in operands)
    return pl.pallas_call(
        body,
        out_shape=list(outs),
        in_specs=[
            SMEM if o.ndim == 1 else HBM if i in far else VMEM for i, o in enumerate(operands)
        ],
        out_specs=[VMEM] * len(outs),
        scratch_shapes=list(scratch),
        compiler_params=pltpu.CompilerParams(vmem_limit_bytes=12 * 1024 * 1024),
        cost_estimate=pl.CostEstimate(flops=flops, bytes_accessed=size, transcendentals=0),
    )(*operands)


def dot(a, b):
    return jnp.dot(a, b, preferred_element_type=F32)


def dot_t(a, b):
    return lax.dot_general(a, b, (((1,), (1,)), ((), ())), preferred_element_type=F32)


def place_of(me):
    index = me[0]
    upper = jnp.where(index >= 6, 1, 0)
    return index & 1, upper, (index - 6 * upper) >> 1


def rows_at(start, count):
    return pl.ds(pl.multiple_of(start, 16), count)


def unpack(wide, a, n_dev, width):
    pieces = width // LANES
    stride = 2 * CAP * pieces
    rows = []
    for j in range(CAP):
        columns = [
            wide[pl.ds((a * CAP + j) * pieces + q, n_dev, stride=stride), :] for q in range(pieces)
        ]
        rows.append(jnp.concatenate(columns, axis=1))
    return jnp.concatenate(rows, axis=0)


def send_body(n_dev, ids_in, gates_in, tokens_in, grad_in, send, picks, ids, gates, tokens, grad, wide, sems):
    moves = [
        pltpu.make_async_copy(source, target, sems.at[i])
        for i, (source, target) in enumerate(
            [(ids_in, ids), (gates_in, gates), (tokens_in, tokens), (grad_in, grad)]
        )
    ]
    for move in moves:
        move.start()
    t, width = tokens.shape
    expert = lax.broadcasted_iota(jnp.int32, (n_dev, t), 0)
    earlier = lax.broadcasted_iota(jnp.int32, (t, t), 0) < lax.broadcasted_iota(jnp.int32, (t, t), 1)
    earlier = jnp.where(earlier, 1.0, 0.0).astype(BF)
    moves[0].wait()
    hot = [jnp.where(expert == ids[k : k + 1, :], 1.0, 0.0) for k in range(2)]
    before = dot((hot[0] + hot[1]).astype(BF), earlier)
    before = [before, before + hot[0]]
    picked = [
        jnp.concatenate(
            [jnp.where(before[k] == float(j), hot[k], 0.0) for j in range(CAP)], axis=0
        )
        for k in range(2)
    ]
    picks[...] = jnp.concatenate(picked, axis=1).astype(BF)
    both = (picked[0] + picked[1]).astype(BF)
    moves[1].wait()
    gate = jnp.sum(picked[0] * gates[0:1, :] + picked[1] * gates[1:2, :], axis=1, keepdims=True)
    pieces = width // LANES
    stride = 2 * CAP * pieces
    for a in range(2):
        moves[2 + a].wait()
        value = dot(both, tokens[...]) if a == 0 else dot(both, grad[...]) * gate
        for j in range(CAP):
            for q in range(pieces):
                wide[pl.ds((a * CAP + j) * pieces + q, n_dev, stride=stride), :] = value[
                    j * n_dev : (j + 1) * n_dev, q * LANES : (q + 1) * LANES
                ]
    send[...] = wide[...].astype(BF)


def product(out, rows_x, rows_g, w_in, w_out, chunk):
    half = w_out.shape[0]
    cut = half // CHUNKS
    a = chunk * cut
    out[:, :cut] = dot(rows_x, w_in[:, a : a + cut]).astype(BF)
    out[:, cut : 2 * cut] = dot(rows_x, w_in[:, half + a : half + a + cut]).astype(BF)
    out[:, 2 * cut :] = dot_t(rows_g, w_out[a : a + cut, :]).astype(BF)


def first_body(n_dev, me, recv, w_in_far, w_out_far, partial, rows, w_in, w_out, wide, sems):
    moves = [
        pltpu.make_async_copy(w_in_far, w_in, sems.at[0]),
        pltpu.make_async_copy(w_out_far, w_out, sems.at[1]),
    ]
    for move in moves:
        move.start()
    wide[...] = recv[...].astype(F32)
    width = w_in.shape[0]
    for a in range(2):
        rows[:, a * width : (a + 1) * width] = unpack(wide, a, n_dev, width).astype(BF)
    count = partial.shape[0]
    other = rows_at((1 - place_of(me)[0]) * count, count)
    for move in moves:
        move.wait()
    product(partial, rows[other, :width], rows[other, width:], w_in, w_out, 0)


def part_body(own, chunk, me, rows, w_in, w_out, partial):
    width = w_in.shape[0]
    count = partial.shape[0]
    core = place_of(me)[0]
    part = rows_at((core if own else 1 - core) * count, count)
    product(partial, rows[part, :width], rows[part, width:], w_in, w_out, chunk)


def third_body(me, mine, from_core, to_after, to_before, total):
    chip = place_of(me)[2]
    count = total.shape[0]

    def two(block):
        block = jnp.where(block >= 3, block - 3, block)
        part = rows_at(block * count, count)
        return mine[part, :].astype(F32) + from_core[part, :].astype(F32)

    to_after[...] = two(chip + 1).astype(BF)
    to_before[...] = two(chip + 2).astype(BF)
    total[...] = two(chip)


def half_body(total, from_before, from_after, to_half, total_out):
    value = total[...] + from_before[...].astype(F32) + from_after[...].astype(F32)
    to_half[...] = value.astype(BF)
    total_out[...] = value


def finish_body(total, from_half, block):
    cut = total.shape[1] // 3
    value = total[...] + from_half[...].astype(F32)
    gate_part, up_part, hidden_grad = value[:, :cut], value[:, cut : 2 * cut], value[:, 2 * cut :]
    sig = jax.nn.sigmoid(gate_part)
    silu = gate_part * sig
    dsilu = sig * (1.0 + gate_part * (1.0 - sig))
    block[:, :cut] = (silu * up_part).astype(BF)
    block[:, cut : 2 * cut] = (hidden_grad * up_part * dsilu).astype(BF)
    block[:, 2 * cut :] = (hidden_grad * silu).astype(BF)


def join_body(*refs):
    out = refs[-1]
    count = refs[0].shape[0]
    for i, ref in enumerate(refs[:-1]):
        out[i * count : (i + 1) * count, :] = ref[...]


def expert_rows(hidden, w_in, w_out, chunk):
    half = w_out.shape[0]
    cut = half // CHUNKS
    a = chunk * cut
    value = dot(hidden[:, :cut], w_out[a : a + cut, :])
    grad = dot_t(hidden[:, cut : 2 * cut], w_in[:, a : a + cut])
    grad = grad + dot_t(hidden[:, 2 * cut :], w_in[:, half + a : half + a + cut])
    return value, grad


def rows_body(chunk, hidden, w_in, w_out, *rest):
    out = rest[-1]
    width = w_in.shape[0]
    value, grad = expert_rows(hidden, w_in, w_out, chunk)
    if chunk:
        value, grad = rest[0][:, :width] + value, rest[0][:, width:] + grad
    out[:, :width] = value
    out[:, width:] = grad


def back_body(n_dev, me, hidden, own_rows, w_in, w_out, *rest):
    send, wide = rest[-2:]
    width = w_in.shape[0]
    value, grad = expert_rows(hidden, w_in, w_out, CHUNKS - 1)
    if CHUNKS > 1:
        value, grad = rest[0][:, :width] + value, rest[0][:, width:] + grad
    core, _, chip = place_of(me)
    pieces = width // LANES
    stride = 2 * CAP * pieces
    count = hidden.shape[0] // 6
    for c in range(2):
        for i in range(6):
            block = chip + i // 2
            block = jnp.where(block >= 3, block - 3, block)
            row = ((core ^ c) * 6 + block * 2 + i % 2) * count
            slot = row // n_dev
            start = (row - slot * n_dev) * stride + slot * pieces
            for a in range(2):
                for q in range(pieces):
                    left = q * LANES
                    if c == 0:
                        left = left + a * width
                        piece = own_rows[i * count : (i + 1) * count, left : left + LANES]
                    else:
                        piece = (value, grad)[a][i * count : (i + 1) * count, left : left + LANES]
                    at = pl.ds(start + a * CAP * pieces + q, count, stride=stride)
                    wide[at, :] = piece
    send[...] = wide[...].astype(BF)


def combine_body(n_dev, recv, picks, ids, gates, tokens, grad_out, moe_out, grad_tokens, wide):
    t, width = tokens.shape
    wide[...] = recv[...].astype(F32)
    back_out = unpack(wide, 0, n_dev, width).astype(BF)
    back_grad = unpack(wide, 1, n_dev, width).astype(BF)
    take = [picks[:, k * t : (k + 1) * t].astype(F32).T.astype(BF) for k in range(2)]
    copied = jnp.sum(jnp.where(ids[...] >= n_dev, gates[...], 0.0), axis=1, keepdims=True)
    moe = gates[:, 0:1] * dot(take[0], back_out) + gates[:, 1:2] * dot(take[1], back_out)
    moe_out[...] = (moe + copied * tokens[...].astype(F32)).astype(BF)
    grad = dot(take[0] + take[1], back_grad)
    grad_tokens[...] = (grad + copied * grad_out[...].astype(F32)).astype(BF)


def per_device(tokens, grad_out, expert_ids, gates, w_in, w_out):
    n_dev = lax.axis_size("expert")
    n_dp = lax.axis_size("dp")
    t, width = tokens.shape
    half = w_out.shape[1]
    count = n_dev * CAP
    wide_rows = 2 * count * width // LANES
    weights = (w_in[0], w_out[0])
    wide = pltpu.VMEM((wide_rows, LANES), F32)
    shape = jax.ShapeDtypeStruct

    me = lax.axis_index("dp").astype(jnp.int32).reshape(1)
    cores = [(i, i ^ 1) for i in range(n_dp)]
    halves = [(i, (i + 6) % n_dp) for i in range(n_dp)]
    after = [(i, i // 6 * 6 + (i + 2) % 6) for i in range(n_dp)]
    before = [(i, i // 6 * 6 + (i + 4) % 6) for i in range(n_dp)]

    send, picks = call(
        functools.partial(send_body, n_dev),
        [shape((wide_rows, LANES), BF), shape((count, 2 * t), BF)],
        [expert_ids.T, gates.T, tokens, grad_out],
        [
            pltpu.VMEM((2, t), jnp.int32),
            pltpu.VMEM((2, t), F32),
            pltpu.VMEM((t, width), BF),
            pltpu.VMEM((t, width), BF),
            wide,
            pltpu.SemaphoreType.DMA((4,)),
        ],
        2 * (2 * count * t * width + n_dev * t * t),
        range(4),
    )

    def exchange(rows):
        parts = rows.reshape(n_dev, wide_rows // n_dev, LANES)
        parts = lax.all_to_all(parts, "expert", split_axis=0, concat_axis=0, tiled=True)
        return parts.reshape(wide_rows, LANES)

    recv = exchange(send)

    cw = 3 * half // CHUNKS
    n_core, n_third = count // 2, count // 6
    flops = 2 * n_core * width * cw
    chunks = range(CHUNKS)
    to_core, rows = call(
        functools.partial(first_body, n_dev),
        [shape((n_core, cw), BF), shape((count, 2 * width), BF)],
        [me, recv, *weights],
        [
            pltpu.VMEM(weights[0].shape, BF),
            pltpu.VMEM(weights[1].shape, BF),
            wide,
            pltpu.SemaphoreType.DMA((2,)),
        ],
        flops,
        (2, 3),
    )

    def part(own, chunk):
        body = functools.partial(part_body, own, chunk)
        return call(body, [shape((n_core, cw), BF)], [me, rows, *weights], (), flops)[0]

    to_core = [to_core] + [part(False, h) for h in chunks[1:]]
    from_core = [lax.ppermute(to_core[h], "dp", cores) for h in chunks]
    mine = [part(True, h) for h in chunks]
    blocks = []
    for h in chunks:
        to_after, to_before, total = call(
            third_body,
            [shape((n_third, cw), BF), shape((n_third, cw), BF), shape((n_third, cw), F32)],
            [me, mine[h], from_core[h]],
        )
        from_before = lax.ppermute(to_after, "dp", after)
        from_after = lax.ppermute(to_before, "dp", before)
        to_half, total = call(
            half_body,
            [shape((n_third, cw), BF), shape((n_third, cw), F32)],
            [total, from_before, from_after],
        )
        from_half = lax.ppermute(to_half, "dp", halves)
        blocks.append(call(finish_body, [shape((n_third, cw), BF)], [total, from_half])[0])
    own_half, other_half = [], []
    for h in chunks:
        of_before = lax.ppermute(blocks[h], "dp", after)
        of_after = lax.ppermute(blocks[h], "dp", before)
        own_half.append(
            call(join_body, [shape((n_core, cw), BF)], [blocks[h], of_after, of_before])[0]
        )
        other_half.append(lax.ppermute(own_half[h], "dp", cores))

    def expert(hidden, upto):
        so_far = []
        for h in range(upto):
            so_far = call(
                functools.partial(rows_body, h),
                [shape((n_core, 2 * width), F32)],
                [hidden[h], *weights, *so_far],
                (),
                flops,
            )
        return so_far

    (send_back,) = call(
        functools.partial(back_body, n_dev),
        [shape((wide_rows, LANES), BF)],
        [me, other_half[-1], *expert(own_half, CHUNKS), *weights, *expert(other_half, CHUNKS - 1)],
        [wide],
        flops,
    )
    recv_back = exchange(send_back)

    moe_out, grad_tokens = call(
        functools.partial(combine_body, n_dev),
        [shape((t, width), BF), shape((t, width), BF)],
        [recv_back, picks, expert_ids, gates, tokens, grad_out],
        [wide],
        2 * 3 * count * t * width,
    )
    return moe_out, grad_tokens


def solution(mesh):
    in_specs = (
        P("expert", "dp"),
        P("expert", "dp"),
        P("expert", None),
        P("expert", None),
        P("expert", "dp", None),
        P("expert", None, "dp"),
    )
    out_specs = (P("expert", "dp"), P("expert", "dp"))
    return jax.shard_map(
        per_device, mesh=mesh, in_specs=in_specs, out_specs=out_specs, check_vma=False
    )
```

time: 165 us -> 143 us (0.87)
  the two profiles are of different devices: /device:TPU:64 before, /device:TPU:257 now
where the time goes in v2:
time: 143 us; the launch traced here: 142 us
  waiting for transfers between devices  80 us (56%)
  starting transfers between devices  48.4 us (34%)
  Pallas kernels  9.29 us (6%)
  local copies, waits for them, and re-layouts  3.58 us (3%)
    all_to_all x2, waiting for transfers between devices, exchange(): lax.all_to_all(parts, 'expert', split_axis=0, concat_axis=0, tiled=True)  52.3 us
    all_to_all x2, starting transfers between devices, exchange(): lax.all_to_all(parts, 'expert', split_axis=0, concat_axis=0, tiled=True)  23.6 us
    ppermute x1, waiting for transfers between devices, per_device(): from_half = lax.ppermute(to_half, 'dp', halves)  12.8 us
    pallas_call x10, Pallas kernels, call(): pl.pallas_call(body, out_shape=list(outs), in_specs=[SMEM if o.ndim == 1...  9.29 us
    ppermute x1, waiting for transfers between devices, per_device(): of_before = lax.ppermute(blocks[h], 'dp', after)  6.32 us
    ppermute x1, starting transfers between devices, per_device(): of_before = lax.ppermute(blocks[h], 'dp', after)  5.91 us
    ppermute x1, starting transfers between devices, per_device(): from_after = lax.ppermute(to_before, 'dp', before)  4.57 us
    ppermute x1, starting transfers between devices, per_device(): of_after = lax.ppermute(blocks[h], 'dp', before)  4.54 us
  transfers between devices with their start and end apart: 9, of which 9 were waited for; matrix products, arithmetic and copies ran while one was open for 0% of the time, Pallas kernels for 1%

profile of v2, /device:TPU:257, one launch (start us, length us, event | category | flops | bytes accessed | tf_op | source)
XLA Modules:
  0.0 142.1 jit_solution(14348678770103057984)
XLA Ops:
  0.6 1.5 %shard_map.77 = (bf16[1536,128]{1,0:T(8,128)(2,1)S(1)}, bf16[192,512]{1,0:T(8,128)(2,1)S(1)}) custom-call(s32[2,256]{1,0:T(2,128)} %bitcast.20, f32[2,256]{1,0:T(2,128)} %bitcast.21, bf16[256,512]{1,0:T(8,128)(2,1)} %tokens.1, bf16[256,512]{1,0:T(8,128)(2,1)} %grad_out.1), custom_call_target="tpu_custom_call" | custom-call | flops 109051904 | bytes 1118208 | tf_op jit(solution)/shard_map/pallas_call | solution.py:27
  2.1 0.0 copy-start.4
  2.1 0.7 copy-done.4
  2.9 0.0 copy-start.5
  2.9 0.7 copy-done.5
  3.6 0.0 copy-start
  3.6 0.0 copy-start.1
  3.6 19.0 %all-to-all-start = ((bf16[64,24,128]{2,1,0:T(8,128)(2,1)}), bf16[64,24,128]{2,1,0:T(8,128)(2,1)S(1)}, u32[]{:S(2)}, u32[]{:S(2)}) async-start(bf16[64,24,128]{2,1,0:T(8,128)(2,1)} %bitcast.19), calls=%async_computation | async-start | bytes 786432 | tf_op jit(solution)/shard_map/all_to_all | solution.py:282
  22.6 27.3 %all-to-all-done = bf16[64,24,128]{2,1,0:T(8,128)(2,1)S(1)} async-done(((bf16[64,24,128]{2,1,0:T(8,128)(2,1)}), bf16[64,24,128]{2,1,0:T(8,128)(2,1)S(1)}, u32[]{:S(2)}, u32[]{:S(2)}) %all-to-all-start) | async-done | bytes 393248 | tf_op jit(solution)/shard_map/all_to_all | solution.py:282
  49.9 2.7 %shard_map.78 = (bf16[96,3072]{1,0:T(8,128)(2,1)S(1)}, bf16[192,1024]{1,0:T(8,128)(2,1)S(1)}) custom-call(s32[1]{0:T(128)} %bitcast.me, bf16[1536,128]{1,0:T(8,128)(2,1)S(1)} %bitcast.18, bf16[512,2048]{1,0:T(8,128)(2,1)} %bitcast.9, bf16[1024,512]{1,0:T(8,128)(2,1)} %bitcast.13), custom_call_target="tpu_custom_call" | custom-call | flops 301989888 | bytes 4521988 | tf_op jit(solution)/shard_map/pallas_call | solution.py:27
  52.6 2.6 %collective-permute-start = (bf16[96,3072]{1,0:T(8,128)(2,1)S(1)}, bf16[96,3072]{1,0:T(8,128)(2,1)S(1)}, u32[]{:S(2)}, u32[]{:S(2)}) collective-permute-start(bf16[96,3072]{1,0:T(8,128)(2,1)S(1)} %get-tuple-element.13), channel_id=1, source_target_pairs={{0,64},{64,0},{128,192},{192,128},{256,320},{320,256},{384,448},{4... | collective-permute-start | bytes 1769480 | tf_op jit(solution)/shard_map/ppermute | solution.py:310
  55.2 0.0 copy-done
  55.2 0.0 copy-done.1
  55.2 0.8 shard_map.79.mine
  56.0 0.8 collective-permute-done.from_core
  56.8 0.1 shard_map.80
  56.9 1.9 %collective-permute-start.1 = (bf16[32,3072]{1,0:T(8,128)(2,1)S(1)}, bf16[32,3072]{1,0:T(8,128)(2,1)S(1)}, u32[]{:S(2)}, u32[]{:S(2)}) collective-permute-start(bf16[32,3072]{1,0:T(8,128)(2,1)S(1)} %get-tuple-element.15), channel_id=1, source_target_pairs={{0,128},{64,192},{128,256},{192,320},{256,0},{320,64},{384,512},{4... | collective-permute-start | bytes 589832 | tf_op jit(solution)/shard_map/ppermute | solution.py:319
  58.9 4.6 %collective-permute-start.2 = (bf16[32,3072]{1,0:T(8,128)(2,1)S(1)}, bf16[32,3072]{1,0:T(8,128)(2,1)S(1)}, u32[]{:S(2)}, u32[]{:S(2)}) collective-permute-start(bf16[32,3072]{1,0:T(8,128)(2,1)S(1)} %get-tuple-element.16), channel_id=1, source_target_pairs={{0,256},{64,320},{128,0},{192,64},{256,128},{320,192},{384,640},{4... | collective-permute-start | bytes 589832 | tf_op jit(solution)/shard_map/ppermute | solution.py:320
  63.4 2.7 %collective-permute-done.1.from_before = bf16[32,3072]{1,0:T(8,128)(2,1)S(1)} collective-permute-done((bf16[32,3072]{1,0:T(8,128)(2,1)S(1)}, bf16[32,3072]{1,0:T(8,128)(2,1)S(1)}, u32[]{:S(2)}, u32[]{:S(2)}) %collective-permute-start.1) | collective-permute-done | bytes 196640 | tf_op jit(solution)/shard_map/ppermute | solution.py:319
  66.1 1.6 %collective-permute-done.2.from_after = bf16[32,3072]{1,0:T(8,128)(2,1)S(1)} collective-permute-done((bf16[32,3072]{1,0:T(8,128)(2,1)S(1)}, bf16[32,3072]{1,0:T(8,128)(2,1)S(1)}, u32[]{:S(2)}, u32[]{:S(2)}) %collective-permute-start.2) | collective-permute-done | bytes 196640 | tf_op jit(solution)/shard_map/ppermute | solution.py:320
  67.7 0.1 shard_map.81
  67.8 1.9 %collective-permute-start.3 = (bf16[32,3072]{1,0:T(8,128)(2,1)S(1)}, bf16[32,3072]{1,0:T(8,128)(2,1)S(1)}, u32[]{:S(2)}, u32[]{:S(2)}) collective-permute-start(bf16[32,3072]{1,0:T(8,128)(2,1)S(1)} %get-tuple-element.18), channel_id=1, source_target_pairs={{0,384},{64,448},{128,512},{192,576},{256,640},{320,704},{384,0},{... | collective-permute-start | bytes 589832 | tf_op jit(solution)/shard_map/ppermute | solution.py:326
  69.7 12.8 %collective-permute-done.3.from_half = bf16[32,3072]{1,0:T(8,128)(2,1)S(1)} collective-permute-done((bf16[32,3072]{1,0:T(8,128)(2,1)S(1)}, bf16[32,3072]{1,0:T(8,128)(2,1)S(1)}, u32[]{:S(2)}, u32[]{:S(2)}) %collective-permute-start.3) | collective-permute-done | bytes 196640 | tf_op jit(solution)/shard_map/ppermute | solution.py:326
  82.5 0.1 shard_map.82.refs_0_
  82.6 4.5 %collective-permute-start.4 = (bf16[32,3072]{1,0:T(8,128)(2,1)S(1)}, bf16[32,3072]{1,0:T(8,128)(2,1)S(1)}, u32[]{:S(2)}, u32[]{:S(2)}) collective-permute-start(bf16[32,3072]{1,0:T(8,128)(2,1)S(1)} %shard_map.82.refs_0_), channel_id=1, source_target_pairs={{0,256},{64,320},{128,0},{192,64},{256,128},{320,192},{384,640},{4... | collective-permute-start | bytes 589832 | tf_op jit(solution)/shard_map/ppermute | solution.py:331
  87.2 5.9 %collective-permute-start.5 = (bf16[32,3072]{1,0:T(8,128)(2,1)S(1)}, bf16[32,3072]{1,0:T(8,128)(2,1)S(1)}, u32[]{:S(2)}, u32[]{:S(2)}) collective-permute-start(bf16[32,3072]{1,0:T(8,128)(2,1)S(1)} %shard_map.82.refs_0_), channel_id=1, source_target_pairs={{0,128},{64,192},{128,256},{192,320},{256,0},{320,64},{384,512},{4... | collective-permute-start | bytes 589832 | tf_op jit(solution)/shard_map/ppermute | solution.py:330
  93.1 2.9 %collective-permute-done.4.refs_1_ = bf16[32,3072]{1,0:T(8,128)(2,1)S(1)} collective-permute-done((bf16[32,3072]{1,0:T(8,128)(2,1)S(1)}, bf16[32,3072]{1,0:T(8,128)(2,1)S(1)}, u32[]{:S(2)}, u32[]{:S(2)}) %collective-permute-start.4) | collective-permute-done | bytes 196640 | tf_op jit(solution)/shard_map/ppermute | solution.py:331
  96.0 6.3 %collective-permute-done.5.refs_2_ = bf16[32,3072]{1,0:T(8,128)(2,1)S(1)} collective-permute-done((bf16[32,3072]{1,0:T(8,128)(2,1)S(1)}, bf16[32,3072]{1,0:T(8,128)(2,1)S(1)}, u32[]{:S(2)}, u32[]{:S(2)}) %collective-permute-start.5) | collective-permute-done | bytes 196640 | tf_op jit(solution)/shard_map/ppermute | solution.py:330
  102.3 3.2 %collective-permute-start.6 = (bf16[96,3072]{1,0:T(8,128)(2,1)S(1)}, bf16[96,3072]{1,0:T(8,128)(2,1)S(1)}, u32[]{:S(2)}, u32[]{:S(2)}) collective-permute-start(bf16[96,3072]{1,0:T(8,128)(2,1)S(1)} %shard_map.83.hidden), channel_id=1, source_target_pairs={{0,64},{64,0},{128,192},{192,128},{256,320},{320,256},{384,448},{4... | collective-permute-start | bytes 1769480 | tf_op jit(solution)/shard_map/ppermute | solution.py:335
  105.6 0.9 shard_map.84.own_rows
  106.5 0.0 copy-start.7
  106.5 0.0 copy-start.8
  106.6 0.0 copy-start.2
  106.6 0.6 collective-permute-done.6.hidden
  107.2 1.7 %shard_map.85 = bf16[1536,128]{1,0:T(8,128)(2,1)} custom-call(s32[1]{0:T(128)} %bitcast.me, bf16[96,3072]{1,0:T(8,128)(2,1)S(1)} %collective-permute-done.6.hidden, f32[96,1024]{1,0:T(8,128)S(1)} %shard_map.84.own_rows, bf16[512,2048]{1,0:T(8,128)(2,1)S(1)} %bitcast.12, bf16[1024,512]{1,0:T(8,128)(2,1)S(1)} %bitcast.16), custom_call_target="tpu_custom_call" | custom-call | flops 301989888 | bytes 4521988 | tf_op jit(solution)/shard_map/pallas_call | solution.py:27
  108.9 4.6 %all-to-all-start.1 = ((bf16[64,24,128]{2,1,0:T(8,128)(2,1)}), bf16[64,24,128]{2,1,0:T(8,128)(2,1)S(1)}, u32[]{:S(2)}, u32[]{:S(2)}) async-start(bf16[64,24,128]{2,1,0:T(8,128)(2,1)} %bitcast.7), calls=%async_computation.1 | async-start | bytes 786432 | tf_op jit(solution)/shard_map/all_to_all | solution.py:282
  113.6 0.0 copy-done.7
  113.6 0.1 copy.8.ids
  113.7 0.0 copy-done.8
  113.7 0.1 copy.9.gates
  113.9 25.0 %all-to-all-done.1 = bf16[64,24,128]{2,1,0:T(8,128)(2,1)S(1)} async-done(((bf16[64,24,128]{2,1,0:T(8,128)(2,1)}), bf16[64,24,128]{2,1,0:T(8,128)(2,1)S(1)}, u32[]{:S(2)}, u32[]{:S(2)}) %all-to-all-start.1) | async-done | bytes 393248 | tf_op jit(solution)/shard_map/all_to_all | solution.py:282
  138.9 0.0 copy-done.2
  138.9 0.0 copy-start.3
  138.9 0.9 copy-done.3
  139.8 0.0 copy-start.6
  139.8 0.9 copy-done.6
  140.7 1.3 shard_map.86
  (1 shorter events, 0.0 us)
Async XLA Ops:
  2.1 0.7 copy-start.4
  2.9 0.7 copy-start.5
  3.6 51.6 %copy-start = (bf16[1,512,2048]{2,1,0:T(8,128)(2,1)S(1)}, bf16[1,512,2048]{2,1,0:T(8,128)(2,1)}, u32[]{:S(2)}) copy-start(bf16[1,512,2048]{2,1,0:T(8,128)(2,1)} %param.10) | copy-start | bytes 6291460
  3.6 51.6 %copy-start.1 = (bf16[1,1024,512]{2,1,0:T(8,128)(2,1)S(1)}, bf16[1,1024,512]{2,1,0:T(8,128)(2,1)}, u32[]{:S(2)}) copy-start(bf16[1,1024,512]{2,1,0:T(8,128)(2,1)} %param.11) | copy-start | bytes 3145732
  3.6 46.3 %all-to-all-start = ((bf16[64,24,128]{2,1,0:T(8,128)(2,1)}), bf16[64,24,128]{2,1,0:T(8,128)(2,1)S(1)}, u32[]{:S(2)}, u32[]{:S(2)}) async-start(bf16[64,24,128]{2,1,0:T(8,128)(2,1)} %bitcast.19), calls=%async_computation | async-start | bytes 786432 | tf_op jit(solution)/shard_map/all_to_all | solution.py:282
  52.6 4.2 %collective-permute-start = (bf16[96,3072]{1,0:T(8,128)(2,1)S(1)}, bf16[96,3072]{1,0:T(8,128)(2,1)S(1)}, u32[]{:S(2)}, u32[]{:S(2)}) collective-permute-start(bf16[96,3072]{1,0:T(8,128)(2,1)S(1)} %get-tuple-element.13), channel_id=1, source_target_pairs={{0,64},{64,0},{128,192},{192,128},{256,320},{320,256},{384,448},{4... | collective-permute-start | bytes 1769480 | tf_op jit(solution)/shard_map/ppermute | solution.py:310
  56.9 9.2 %collective-permute-start.1 = (bf16[32,3072]{1,0:T(8,128)(2,1)S(1)}, bf16[32,3072]{1,0:T(8,128)(2,1)S(1)}, u32[]{:S(2)}, u32[]{:S(2)}) collective-permute-start(bf16[32,3072]{1,0:T(8,128)(2,1)S(1)} %get-tuple-element.15), channel_id=1, source_target_pairs={{0,128},{64,192},{128,256},{192,320},{256,0},{320,64},{384,512},{4... | collective-permute-start | bytes 589832 | tf_op jit(solution)/shard_map/ppermute | solution.py:319
  58.9 8.9 %collective-permute-start.2 = (bf16[32,3072]{1,0:T(8,128)(2,1)S(1)}, bf16[32,3072]{1,0:T(8,128)(2,1)S(1)}, u32[]{:S(2)}, u32[]{:S(2)}) collective-permute-start(bf16[32,3072]{1,0:T(8,128)(2,1)S(1)} %get-tuple-element.16), channel_id=1, source_target_pairs={{0,256},{64,320},{128,0},{192,64},{256,128},{320,192},{384,640},{4... | collective-permute-start | bytes 589832 | tf_op jit(solution)/shard_map/ppermute | solution.py:320
  67.8 14.7 %collective-permute-start.3 = (bf16[32,3072]{1,0:T(8,128)(2,1)S(1)}, bf16[32,3072]{1,0:T(8,128)(2,1)S(1)}, u32[]{:S(2)}, u32[]{:S(2)}) collective-permute-start(bf16[32,3072]{1,0:T(8,128)(2,1)S(1)} %get-tuple-element.18), channel_id=1, source_target_pairs={{0,384},{64,448},{128,512},{192,576},{256,640},{320,704},{384,0},{... | collective-permute-start | bytes 589832 | tf_op jit(solution)/shard_map/ppermute | solution.py:326
  82.6 13.4 %collective-permute-start.4 = (bf16[32,3072]{1,0:T(8,128)(2,1)S(1)}, bf16[32,3072]{1,0:T(8,128)(2,1)S(1)}, u32[]{:S(2)}, u32[]{:S(2)}) collective-permute-start(bf16[32,3072]{1,0:T(8,128)(2,1)S(1)} %shard_map.82.refs_0_), channel_id=1, source_target_pairs={{0,256},{64,320},{128,0},{192,64},{256,128},{320,192},{384,640},{4... | collective-permute-start | bytes 589832 | tf_op jit(solution)/shard_map/ppermute | solution.py:331
  87.2 15.1 %collective-permute-start.5 = (bf16[32,3072]{1,0:T(8,128)(2,1)S(1)}, bf16[32,3072]{1,0:T(8,128)(2,1)S(1)}, u32[]{:S(2)}, u32[]{:S(2)}) collective-permute-start(bf16[32,3072]{1,0:T(8,128)(2,1)S(1)} %shard_map.82.refs_0_), channel_id=1, source_target_pairs={{0,128},{64,192},{128,256},{192,320},{256,0},{320,64},{384,512},{4... | collective-permute-start | bytes 589832 | tf_op jit(solution)/shard_map/ppermute | solution.py:330
  102.3 4.9 %collective-permute-start.6 = (bf16[96,3072]{1,0:T(8,128)(2,1)S(1)}, bf16[96,3072]{1,0:T(8,128)(2,1)S(1)}, u32[]{:S(2)}, u32[]{:S(2)}) collective-permute-start(bf16[96,3072]{1,0:T(8,128)(2,1)S(1)} %shard_map.83.hidden), channel_id=1, source_target_pairs={{0,64},{64,0},{128,192},{192,128},{256,320},{320,256},{384,448},{4... | collective-permute-start | bytes 1769480 | tf_op jit(solution)/shard_map/ppermute | solution.py:335
  106.5 7.1 %copy-start.7 = (s32[256,2]{0,1:T(2,128)S(1)}, s32[256,2]{0,1:T(2,128)}, u32[]{:S(2)}) copy-start(s32[256,2]{0,1:T(2,128)} %param.8) | copy-start | bytes 6148
  106.5 7.2 %copy-start.8 = (f32[256,2]{0,1:T(2,128)S(1)}, f32[256,2]{0,1:T(2,128)}, u32[]{:S(2)}) copy-start(f32[256,2]{0,1:T(2,128)} %param.9) | copy-start | bytes 6148
  106.6 32.3 %copy-start.2 = (bf16[256,512]{1,0:T(8,128)(2,1)S(1)}, bf16[256,512]{1,0:T(8,128)(2,1)}, u32[]{:S(2)}) copy-start(bf16[256,512]{1,0:T(8,128)(2,1)} %tokens.1) | copy-start | bytes 786436
  108.9 29.9 %all-to-all-start.1 = ((bf16[64,24,128]{2,1,0:T(8,128)(2,1)}), bf16[64,24,128]{2,1,0:T(8,128)(2,1)S(1)}, u32[]{:S(2)}, u32[]{:S(2)}) async-start(bf16[64,24,128]{2,1,0:T(8,128)(2,1)} %bitcast.7), calls=%async_computation.1 | async-start | bytes 786432 | tf_op jit(solution)/shard_map/all_to_all | solution.py:282
  138.9 1.0 copy-start.3
  139.8 0.9 copy-start.6

commit v3 on v2

--- a/solution.py
+++ b/solution.py
@@ -18,19 +18,19 @@
 
 
 def call(body, outs, operands, scratch=(), flops=0, far=()):
+    out_far = [i for i, o in enumerate(outs) if not isinstance(o, jax.ShapeDtypeStruct)]
     operands = [
         pltpu.with_memory_space_constraint(o, pltpu.HBM) if i in far else o
         for i, o in enumerate(operands)
     ]
-    size = sum(o.size * o.dtype.itemsize for o in outs)
-    size += sum(o.size * o.dtype.itemsize for o in operands)
+    size = sum(o.size * o.dtype.itemsize for o in operands)
     return pl.pallas_call(
         body,
         out_shape=list(outs),
         in_specs=[
             SMEM if o.ndim == 1 else HBM if i in far else VMEM for i, o in enumerate(operands)
         ],
-        out_specs=[VMEM] * len(outs),
+        out_specs=[HBM if i in out_far else VMEM for i in range(len(outs))],
         scratch_shapes=list(scratch),
         compiler_params=pltpu.CompilerParams(vmem_limit_bytes=12 * 1024 * 1024),
         cost_estimate=pl.CostEstimate(flops=flops, bytes_accessed=size, transcendentals=0),
@@ -67,15 +67,20 @@
     return jnp.concatenate(rows, axis=0)
 
 
-def send_body(n_dev, ids_in, gates_in, tokens_in, grad_in, send, picks, ids, gates, tokens, grad, wide, sems):
+def started(sources, targets, sems):
     moves = [
         pltpu.make_async_copy(source, target, sems.at[i])
-        for i, (source, target) in enumerate(
-            [(ids_in, ids), (gates_in, gates), (tokens_in, tokens), (grad_in, grad)]
-        )
+        for i, (source, target) in enumerate(zip(sources, targets))
     ]
     for move in moves:
         move.start()
+    return moves
+
+
+def send_body(n_dev, *refs):
+    send_out, picks_out, weigh_out, w_in, w_out, *rest = refs[6:]
+    send, picks, weigh, ids, gates, tokens, grad, wide, sems, out_sems = rest
+    moves = started(refs[:6], (ids, gates, tokens, grad, w_in, w_out), sems)
     t, width = tokens.shape
     expert = lax.broadcasted_iota(jnp.int32, (n_dev, t), 0)
     earlier = lax.broadcasted_iota(jnp.int32, (t, t), 0) < lax.broadcasted_iota(jnp.int32, (t, t), 1)
@@ -91,9 +96,14 @@
         for k in range(2)
     ]
     picks[...] = jnp.concatenate(picked, axis=1).astype(BF)
+    outs = started((picks,), (picks_out,), out_sems)
     both = (picked[0] + picked[1]).astype(BF)
     moves[1].wait()
     gate = jnp.sum(picked[0] * gates[0:1, :] + picked[1] * gates[1:2, :], axis=1, keepdims=True)
+    copied = jnp.sum(jnp.where(ids[...] >= n_dev, gates[...], 0.0), axis=0, keepdims=True)
+    lines = [gates[...], copied, jnp.zeros((5, t), F32)]
+    weigh[...] = jnp.concatenate(lines, axis=0).T
+    outs += started((weigh,), (weigh_out,), out_sems.at[pl.ds(1, 1)])
     pieces = width // LANES
     stride = 2 * CAP * pieces
     for a in range(2):
@@ -104,7 +114,13 @@
                 wide[pl.ds((a * CAP + j) * pieces + q, n_dev, stride=stride), :] = value[
                     j * n_dev : (j + 1) * n_dev, q * LANES : (q + 1) * LANES
                 ]
-    send[...] = wide[...].astype(BF)
+    part = wide.shape[0] // 4
+    for i in range(4):
+        rows = pl.ds(i * part, part)
+        send[rows, :] = wide[rows, :].astype(BF)
+        outs += started((send.at[rows],), (send_out.at[rows],), out_sems.at[pl.ds(2 + i, 1)])
+    for move in moves[4:] + outs:
+        move.wait()
 
 
 def product(out, rows_x, rows_g, w_in, w_out, chunk):
@@ -116,21 +132,13 @@
     out[:, 2 * cut :] = dot_t(rows_g, w_out[a : a + cut, :]).astype(BF)
 
 
-def first_body(n_dev, me, recv, w_in_far, w_out_far, partial, rows, w_in, w_out, wide, sems):
-    moves = [
-        pltpu.make_async_copy(w_in_far, w_in, sems.at[0]),
-        pltpu.make_async_copy(w_out_far, w_out, sems.at[1]),
-    ]
-    for move in moves:
-        move.start()
+def first_body(n_dev, me, recv, w_in, w_out, partial, rows, wide):
     wide[...] = recv[...].astype(F32)
     width = w_in.shape[0]
     for a in range(2):
         rows[:, a * width : (a + 1) * width] = unpack(wide, a, n_dev, width).astype(BF)
     count = partial.shape[0]
     other = rows_at((1 - place_of(me)[0]) * count, count)
-    for move in moves:
-        move.wait()
     product(partial, rows[other, :width], rows[other, width:], w_in, w_out, 0)
 
 
@@ -231,16 +239,20 @@
     send[...] = wide[...].astype(BF)
 
 
-def combine_body(n_dev, recv, picks, ids, gates, tokens, grad_out, moe_out, grad_tokens, wide):
+def combine_body(n_dev, recv, picks, weigh, *refs):
+    moe_out, grad_tokens, tokens, grad_out, wide, sems = refs[2:]
+    moves = started(refs[:2], (tokens, grad_out), sems)
     t, width = tokens.shape
     wide[...] = recv[...].astype(F32)
     back_out = unpack(wide, 0, n_dev, width).astype(BF)
     back_grad = unpack(wide, 1, n_dev, width).astype(BF)
     take = [picks[:, k * t : (k + 1) * t].astype(F32).T.astype(BF) for k in range(2)]
-    copied = jnp.sum(jnp.where(ids[...] >= n_dev, gates[...], 0.0), axis=1, keepdims=True)
-    moe = gates[:, 0:1] * dot(take[0], back_out) + gates[:, 1:2] * dot(take[1], back_out)
+    copied = weigh[:, 2:3]
+    moe = weigh[:, 0:1] * dot(take[0], back_out) + weigh[:, 1:2] * dot(take[1], back_out)
+    moves[0].wait()
     moe_out[...] = (moe + copied * tokens[...].astype(F32)).astype(BF)
     grad = dot(take[0] + take[1], back_grad)
+    moves[1].wait()
     grad_tokens[...] = (grad + copied * grad_out[...].astype(F32)).astype(BF)
 
 
@@ -251,7 +263,6 @@
     half = w_out.shape[1]
     count = n_dev * CAP
     wide_rows = 2 * count * width // LANES
-    weights = (w_in[0], w_out[0])
     wide = pltpu.VMEM((wide_rows, LANES), F32)
     shape = jax.ShapeDtypeStruct
 
@@ -261,20 +272,30 @@
     after = [(i, i // 6 * 6 + (i + 2) % 6) for i in range(n_dp)]
     before = [(i, i // 6 * 6 + (i + 4) % 6) for i in range(n_dp)]
 
-    send, picks = call(
+    send, picks, weigh, *weights = call(
         functools.partial(send_body, n_dev),
-        [shape((wide_rows, LANES), BF), shape((count, 2 * t), BF)],
-        [expert_ids.T, gates.T, tokens, grad_out],
         [
+            pltpu.HBM((wide_rows, LANES), BF),
+            pltpu.HBM((count, 2 * t), BF),
+            pltpu.HBM((t, 8), F32),
+            shape(w_in.shape[1:], BF),
+            shape(w_out.shape[1:], BF),
+        ],
+        [expert_ids.T, gates.T, tokens, grad_out, w_in[0], w_out[0]],
+        [
+            pltpu.VMEM((wide_rows, LANES), BF),
+            pltpu.VMEM((count, 2 * t), BF),
+            pltpu.VMEM((t, 8), F32),
             pltpu.VMEM((2, t), jnp.int32),
             pltpu.VMEM((2, t), F32),
             pltpu.VMEM((t, width), BF),
             pltpu.VMEM((t, width), BF),
             wide,
-            pltpu.SemaphoreType.DMA((4,)),
+            pltpu.SemaphoreType.DMA((6,)),
+            pltpu.SemaphoreType.DMA((6,)),
         ],
         2 * (2 * count * t * width + n_dev * t * t),
-        range(4),
+        range(6),
     )
 
     def exchange(rows):
@@ -292,14 +313,8 @@
         functools.partial(first_body, n_dev),
         [shape((n_core, cw), BF), shape((count, 2 * width), BF)],
         [me, recv, *weights],
-        [
-            pltpu.VMEM(weights[0].shape, BF),
-            pltpu.VMEM(weights[1].shape, BF),
-            wide,
-            pltpu.SemaphoreType.DMA((2,)),
-        ],
+        [wide],
         flops,
-        (2, 3),
     )
 
     def part(own, chunk):
@@ -358,9 +373,15 @@
     moe_out, grad_tokens = call(
         functools.partial(combine_body, n_dev),
         [shape((t, width), BF), shape((t, width), BF)],
-        [recv_back, picks, expert_ids, gates, tokens, grad_out],
-        [wide],
+        [recv_back, picks, weigh, tokens, grad_out],
+        [
+            pltpu.VMEM((t, width), BF),
+            pltpu.VMEM((t, width), BF),
+            wide,
+            pltpu.SemaphoreType.DMA((2,)),
+        ],
         2 * 3 * count * t * width,
+        (3, 4),
     )
     return moe_out, grad_tokens
 

time: 143 us -> 138 us (0.965)
  the two profiles are of different devices: /device:TPU:257 before, /device:TPU:64 now
where the time goes in v3:
time: 138 us
  waiting for transfers between devices  51.4 us (37%)
  starting transfers between devices  48.1 us (35%)
  blocking collectives  29.2 us (21%)
  Pallas kernels  8.55 us (6%)
    all_to_all x1, blocking collectives, exchange(): lax.all_to_all(parts, 'expert', split_axis=0, concat_axis=0, tiled=True)  29.2 us
    all_to_all x1, waiting for transfers between devices, exchange(): lax.all_to_all(parts, 'expert', split_axis=0, concat_axis=0, tiled=True)  27 us
    all_to_all x1, starting transfers between devices, exchange(): lax.all_to_all(parts, 'expert', split_axis=0, concat_axis=0, tiled=True)  22.4 us
    ppermute x1, waiting for transfers between devices, per_device(): from_half = lax.ppermute(to_half, 'dp', halves)  8.77 us
    pallas_call x10, Pallas kernels, call(): pl.pallas_call(body, out_shape=list(outs), in_specs=[SMEM if o.ndim == 1...  8.55 us
    ppermute x1, starting transfers between devices, per_device(): of_before = lax.ppermute(blocks[h], 'dp', after)  6.74 us
    ppermute x1, starting transfers between devices, per_device(): from_half = lax.ppermute(to_half, 'dp', halves)  6.66 us
    ppermute x1, waiting for transfers between devices, per_device(): of_after = lax.ppermute(blocks[h], 'dp', before)  5.43 us
  transfers between devices with their start and end apart: 8, of which 8 were waited for; matrix products, arithmetic and copies ran while one was open for 0% of the time, Pallas kernels for 1%

profile of v3, /device:TPU:64, one launch (start us, length us, event | category | flops | bytes accessed | tf_op | source)
XLA Modules:
  0.0 138.0 jit_solution(4191503300947627807)
XLA Ops:
  0.6 2.3 %shard_map.77 = (bf16[1536,128]{1,0:T(8,128)(2,1)}, bf16[192,512]{1,0:T(8,128)(2,1)}, f32[256,8]{1,0:T(8,128)}, bf16[512,2048]{1,0:T(8,128)(2,1)S(1)}, bf16[1024,512]{1,0:T(8,128)(2,1)S(1)}) custom-call(s32[2,256]{1,0:T(2,128)} %bitcast.15, f32[2,256]{1,0:T(2,128)} %bitcast.16, bf16[256,512]{1,0:T(8,128)(2,1)} %refs_0_.1, bf16[256,512]{1,0:T(8,128)(2,1)} %refs_1_.1, ...), custom_call_target="tpu_custom_call" | custom-call | flops 109051904 | bytes 3674112 | tf_op jit(solution)/shard_map/pallas_call | solution.py:27
  3.0 22.4 %all-to-all-start = ((bf16[64,24,128]{2,1,0:T(8,128)(2,1)}), bf16[64,24,128]{2,1,0:T(8,128)(2,1)S(1)}, u32[]{:S(2)}, u32[]{:S(2)}) async-start(bf16[64,24,128]{2,1,0:T(8,128)(2,1)} %bitcast.14), calls=%async_computation | async-start | bytes 786432 | tf_op jit(solution)/shard_map/all_to_all | solution.py:303
  25.3 27.0 %all-to-all-done = bf16[64,24,128]{2,1,0:T(8,128)(2,1)S(1)} async-done(((bf16[64,24,128]{2,1,0:T(8,128)(2,1)}), bf16[64,24,128]{2,1,0:T(8,128)(2,1)S(1)}, u32[]{:S(2)}, u32[]{:S(2)}) %all-to-all-start) | async-done | bytes 393248 | tf_op jit(solution)/shard_map/all_to_all | solution.py:303
  52.3 0.9 shard_map.78
  53.1 1.9 %collective-permute-start = (bf16[96,3072]{1,0:T(8,128)(2,1)S(1)}, bf16[96,3072]{1,0:T(8,128)(2,1)S(1)}, u32[]{:S(2)}, u32[]{:S(2)}) collective-permute-start(bf16[96,3072]{1,0:T(8,128)(2,1)S(1)} %get-tuple-element.18), channel_id=1, source_target_pairs={{0,64},{64,0},{128,192},{192,128},{256,320},{320,256},{384,448},{4... | collective-permute-start | bytes 1769480 | tf_op jit(solution)/shard_map/ppermute | solution.py:325
  55.1 0.8 shard_map.79.mine
  55.9 1.2 collective-permute-done.from_core
  57.0 0.1 shard_map.80
  57.2 1.9 %collective-permute-start.1 = (bf16[32,3072]{1,0:T(8,128)(2,1)S(1)}, bf16[32,3072]{1,0:T(8,128)(2,1)S(1)}, u32[]{:S(2)}, u32[]{:S(2)}) collective-permute-start(bf16[32,3072]{1,0:T(8,128)(2,1)S(1)} %get-tuple-element.20), channel_id=1, source_target_pairs={{0,128},{64,192},{128,256},{192,320},{256,0},{320,64},{384,512},{4... | collective-permute-start | bytes 589832 | tf_op jit(solution)/shard_map/ppermute | solution.py:334
  59.1 3.9 %collective-permute-start.2 = (bf16[32,3072]{1,0:T(8,128)(2,1)S(1)}, bf16[32,3072]{1,0:T(8,128)(2,1)S(1)}, u32[]{:S(2)}, u32[]{:S(2)}) collective-permute-start(bf16[32,3072]{1,0:T(8,128)(2,1)S(1)} %get-tuple-element.21), channel_id=1, source_target_pairs={{0,256},{64,320},{128,0},{192,64},{256,128},{320,192},{384,640},{4... | collective-permute-start | bytes 589832 | tf_op jit(solution)/shard_map/ppermute | solution.py:335
  63.0 3.8 %collective-permute-done.1.from_before = bf16[32,3072]{1,0:T(8,128)(2,1)S(1)} collective-permute-done((bf16[32,3072]{1,0:T(8,128)(2,1)S(1)}, bf16[32,3072]{1,0:T(8,128)(2,1)S(1)}, u32[]{:S(2)}, u32[]{:S(2)}) %collective-permute-start.1) | collective-permute-done | bytes 196640 | tf_op jit(solution)/shard_map/ppermute | solution.py:334
  66.8 1.1 collective-permute-done.2.from_after
  67.9 0.1 shard_map.81
  68.0 6.7 %collective-permute-start.3 = (bf16[32,3072]{1,0:T(8,128)(2,1)S(1)}, bf16[32,3072]{1,0:T(8,128)(2,1)S(1)}, u32[]{:S(2)}, u32[]{:S(2)}) collective-permute-start(bf16[32,3072]{1,0:T(8,128)(2,1)S(1)} %get-tuple-element.23), channel_id=1, source_target_pairs={{0,384},{64,448},{128,512},{192,576},{256,640},{320,704},{384,0},{... | collective-permute-start | bytes 589832 | tf_op jit(solution)/shard_map/ppermute | solution.py:341
  74.7 8.8 %collective-permute-done.3.from_half = bf16[32,3072]{1,0:T(8,128)(2,1)S(1)} collective-permute-done((bf16[32,3072]{1,0:T(8,128)(2,1)S(1)}, bf16[32,3072]{1,0:T(8,128)(2,1)S(1)}, u32[]{:S(2)}, u32[]{:S(2)}) %collective-permute-start.3) | collective-permute-done | bytes 196640 | tf_op jit(solution)/shard_map/ppermute | solution.py:341
  83.5 0.1 shard_map.82.refs_0_
  83.5 6.7 %collective-permute-start.5 = (bf16[32,3072]{1,0:T(8,128)(2,1)S(1)}, bf16[32,3072]{1,0:T(8,128)(2,1)S(1)}, u32[]{:S(2)}, u32[]{:S(2)}) collective-permute-start(bf16[32,3072]{1,0:T(8,128)(2,1)S(1)} %shard_map.82.refs_0_), channel_id=1, source_target_pairs={{0,128},{64,192},{128,256},{192,320},{256,0},{320,64},{384,512},{4... | collective-permute-start | bytes 589832 | tf_op jit(solution)/shard_map/ppermute | solution.py:345
  90.3 2.7 %collective-permute-start.4 = (bf16[32,3072]{1,0:T(8,128)(2,1)S(1)}, bf16[32,3072]{1,0:T(8,128)(2,1)S(1)}, u32[]{:S(2)}, u32[]{:S(2)}) collective-permute-start(bf16[32,3072]{1,0:T(8,128)(2,1)S(1)} %shard_map.82.refs_0_), channel_id=1, source_target_pairs={{0,256},{64,320},{128,0},{192,64},{256,128},{320,192},{384,640},{4... | collective-permute-start | bytes 589832 | tf_op jit(solution)/shard_map/ppermute | solution.py:346
  93.0 3.1 %collective-permute-done.5.refs_2_ = bf16[32,3072]{1,0:T(8,128)(2,1)S(1)} collective-permute-done((bf16[32,3072]{1,0:T(8,128)(2,1)S(1)}, bf16[32,3072]{1,0:T(8,128)(2,1)S(1)}, u32[]{:S(2)}, u32[]{:S(2)}) %collective-permute-start.5) | collective-permute-done | bytes 196640 | tf_op jit(solution)/shard_map/ppermute | solution.py:345
  96.1 5.4 %collective-permute-done.4.refs_1_ = bf16[32,3072]{1,0:T(8,128)(2,1)S(1)} collective-permute-done((bf16[32,3072]{1,0:T(8,128)(2,1)S(1)}, bf16[32,3072]{1,0:T(8,128)(2,1)S(1)}, u32[]{:S(2)}, u32[]{:S(2)}) %collective-permute-start.4) | collective-permute-done | bytes 196640 | tf_op jit(solution)/shard_map/ppermute | solution.py:346
  101.6 1.9 %collective-permute-start.6 = (bf16[96,3072]{1,0:T(8,128)(2,1)S(1)}, bf16[96,3072]{1,0:T(8,128)(2,1)S(1)}, u32[]{:S(2)}, u32[]{:S(2)}) collective-permute-start(bf16[96,3072]{1,0:T(8,128)(2,1)S(1)} %shard_map.83.hidden), channel_id=1, source_target_pairs={{0,64},{64,0},{128,192},{192,128},{256,320},{320,256},{384,448},{4... | collective-permute-start | bytes 1769480 | tf_op jit(solution)/shard_map/ppermute | solution.py:350
  103.5 0.9 shard_map.84.own_rows
  104.4 0.0 copy-start
  104.5 0.0 copy-start.1
  104.5 1.0 collective-permute-done.6.hidden
  105.5 1.0 shard_map.85
  106.5 29.2 %all_to_all.10 = bf16[64,24,128]{2,1,0:T(8,128)(2,1)S(1)} all-to-all(bf16[64,24,128]{2,1,0:T(8,128)(2,1)S(1)} %bitcast.10), channel_id=1, replica_groups=mesh['dp'=12,'expert'=64] {'expert'}, dimensions={0} | all-to-all | bytes 786432 | tf_op jit(solution)/shard_map/all_to_all | solution.py:303
  135.7 0.0 copy-done
  135.7 0.0 copy-done.1
  135.7 2.3 %shard_map.86 = (bf16[256,512]{1,0:T(8,128)(2,1)}, bf16[256,512]{1,0:T(8,128)(2,1)}) custom-call(bf16[1536,128]{1,0:T(8,128)(2,1)S(1)} %bitcast.9, bf16[192,512]{1,0:T(8,128)(2,1)S(1)} %copy-done, f32[256,8]{1,0:T(8,128)S(1)} %copy-done.1, bf16[256,512]{1,0:T(8,128)(2,1)} %refs_0_.1, bf16[256,512]{1,0:T(8,128)(2,1)} %refs_1_.1), custom_call_target="tpu_custom_call" | custom-call | flops 150994944 | bytes 1122304 | tf_op jit(solution)/shard_map/pallas_call | solution.py:27
  (1 shorter events, 0.0 us)
Async XLA Ops:
  3.0 49.3 %all-to-all-start = ((bf16[64,24,128]{2,1,0:T(8,128)(2,1)}), bf16[64,24,128]{2,1,0:T(8,128)(2,1)S(1)}, u32[]{:S(2)}, u32[]{:S(2)}) async-start(bf16[64,24,128]{2,1,0:T(8,128)(2,1)} %bitcast.14), calls=%async_computation | async-start | bytes 786432 | tf_op jit(solution)/shard_map/all_to_all | solution.py:303
  53.1 3.9 %collective-permute-start = (bf16[96,3072]{1,0:T(8,128)(2,1)S(1)}, bf16[96,3072]{1,0:T(8,128)(2,1)S(1)}, u32[]{:S(2)}, u32[]{:S(2)}) collective-permute-start(bf16[96,3072]{1,0:T(8,128)(2,1)S(1)} %get-tuple-element.18), channel_id=1, source_target_pairs={{0,64},{64,0},{128,192},{192,128},{256,320},{320,256},{384,448},{4... | collective-permute-start | bytes 1769480 | tf_op jit(solution)/shard_map/ppermute | solution.py:325
  57.2 9.6 %collective-permute-start.1 = (bf16[32,3072]{1,0:T(8,128)(2,1)S(1)}, bf16[32,3072]{1,0:T(8,128)(2,1)S(1)}, u32[]{:S(2)}, u32[]{:S(2)}) collective-permute-start(bf16[32,3072]{1,0:T(8,128)(2,1)S(1)} %get-tuple-element.20), channel_id=1, source_target_pairs={{0,128},{64,192},{128,256},{192,320},{256,0},{320,64},{384,512},{4... | collective-permute-start | bytes 589832 | tf_op jit(solution)/shard_map/ppermute | solution.py:334
  59.1 8.8 %collective-permute-start.2 = (bf16[32,3072]{1,0:T(8,128)(2,1)S(1)}, bf16[32,3072]{1,0:T(8,128)(2,1)S(1)}, u32[]{:S(2)}, u32[]{:S(2)}) collective-permute-start(bf16[32,3072]{1,0:T(8,128)(2,1)S(1)} %get-tuple-element.21), channel_id=1, source_target_pairs={{0,256},{64,320},{128,0},{192,64},{256,128},{320,192},{384,640},{4... | collective-permute-start | bytes 589832 | tf_op jit(solution)/shard_map/ppermute | solution.py:335
  68.0 15.4 %collective-permute-start.3 = (bf16[32,3072]{1,0:T(8,128)(2,1)S(1)}, bf16[32,3072]{1,0:T(8,128)(2,1)S(1)}, u32[]{:S(2)}, u32[]{:S(2)}) collective-permute-start(bf16[32,3072]{1,0:T(8,128)(2,1)S(1)} %get-tuple-element.23), channel_id=1, source_target_pairs={{0,384},{64,448},{128,512},{192,576},{256,640},{320,704},{384,0},{... | collective-permute-start | bytes 589832 | tf_op jit(solution)/shard_map/ppermute | solution.py:341
  83.5 12.6 %collective-permute-start.5 = (bf16[32,3072]{1,0:T(8,128)(2,1)S(1)}, bf16[32,3072]{1,0:T(8,128)(2,1)S(1)}, u32[]{:S(2)}, u32[]{:S(2)}) collective-permute-start(bf16[32,3072]{1,0:T(8,128)(2,1)S(1)} %shard_map.82.refs_0_), channel_id=1, source_target_pairs={{0,128},{64,192},{128,256},{192,320},{256,0},{320,64},{384,512},{4... | collective-permute-start | bytes 589832 | tf_op jit(solution)/shard_map/ppermute | solution.py:345
  90.3 11.2 %collective-permute-start.4 = (bf16[32,3072]{1,0:T(8,128)(2,1)S(1)}, bf16[32,3072]{1,0:T(8,128)(2,1)S(1)}, u32[]{:S(2)}, u32[]{:S(2)}) collective-permute-start(bf16[32,3072]{1,0:T(8,128)(2,1)S(1)} %shard_map.82.refs_0_), channel_id=1, source_target_pairs={{0,256},{64,320},{128,0},{192,64},{256,128},{320,192},{384,640},{4... | collective-permute-start | bytes 589832 | tf_op jit(solution)/shard_map/ppermute | solution.py:346
  101.6 3.9 %collective-permute-start.6 = (bf16[96,3072]{1,0:T(8,128)(2,1)S(1)}, bf16[96,3072]{1,0:T(8,128)(2,1)S(1)}, u32[]{:S(2)}, u32[]{:S(2)}) collective-permute-start(bf16[96,3072]{1,0:T(8,128)(2,1)S(1)} %shard_map.83.hidden), channel_id=1, source_target_pairs={{0,64},{64,0},{128,192},{192,128},{256,320},{320,256},{384,448},{4... | collective-permute-start | bytes 1769480 | tf_op jit(solution)/shard_map/ppermute | solution.py:350
  104.4 31.2 %copy-start = (bf16[192,512]{1,0:T(8,128)(2,1)S(1)}, bf16[192,512]{1,0:T(8,128)(2,1)}, u32[]{:S(2)}) copy-start(bf16[192,512]{1,0:T(8,128)(2,1)} %get-tuple-element.24.picks) | copy-start | bytes 589828
  104.5 31.2 %copy-start.1 = (f32[256,8]{1,0:T(8,128)S(1)}, f32[256,8]{1,0:T(8,128)}, u32[]{:S(2)}) copy-start(f32[256,8]{1,0:T(8,128)} %get-tuple-element.25.weigh) | copy-start | bytes 24580

commit v4 on v3

--- a/solution.py
+++ b/solution.py
@@ -95,7 +95,8 @@
         )
         for k in range(2)
     ]
-    picks[...] = jnp.concatenate(picked, axis=1).astype(BF)
+    for k in range(2):
+        picks[:, k * CAP * n_dev : (k + 1) * CAP * n_dev] = picked[k].T.astype(BF)
     outs = started((picks,), (picks_out,), out_sems)
     both = (picked[0] + picked[1]).astype(BF)
     moves[1].wait()
@@ -199,14 +200,14 @@
     return value, grad
 
 
-def rows_body(chunk, hidden, w_in, w_out, *rest):
-    out = rest[-1]
+def rows_body(hidden, w_in, w_out, tokens_in, grad_in, out, tokens, grad_out, sems):
+    moves = started((tokens_in, grad_in), (tokens, grad_out), sems)
     width = w_in.shape[0]
-    value, grad = expert_rows(hidden, w_in, w_out, chunk)
-    if chunk:
-        value, grad = rest[0][:, :width] + value, rest[0][:, width:] + grad
+    value, grad = expert_rows(hidden, w_in, w_out, 0)
     out[:, :width] = value
     out[:, width:] = grad
+    for move in moves:
+        move.wait()
 
 
 def back_body(n_dev, me, hidden, own_rows, w_in, w_out, *rest):
@@ -239,20 +240,17 @@
     send[...] = wide[...].astype(BF)
 
 
-def combine_body(n_dev, recv, picks, weigh, *refs):
-    moe_out, grad_tokens, tokens, grad_out, wide, sems = refs[2:]
-    moves = started(refs[:2], (tokens, grad_out), sems)
+def combine_body(n_dev, recv, picks, weigh, tokens, grad_out, moe_out, grad_tokens, wide):
     t, width = tokens.shape
     wide[...] = recv[...].astype(F32)
     back_out = unpack(wide, 0, n_dev, width).astype(BF)
     back_grad = unpack(wide, 1, n_dev, width).astype(BF)
-    take = [picks[:, k * t : (k + 1) * t].astype(F32).T.astype(BF) for k in range(2)]
+    count = CAP * n_dev
+    take = [picks[:, :count], picks[:, count:]]
     copied = weigh[:, 2:3]
     moe = weigh[:, 0:1] * dot(take[0], back_out) + weigh[:, 1:2] * dot(take[1], back_out)
-    moves[0].wait()
     moe_out[...] = (moe + copied * tokens[...].astype(F32)).astype(BF)
     grad = dot(take[0] + take[1], back_grad)
-    moves[1].wait()
     grad_tokens[...] = (grad + copied * grad_out[...].astype(F32)).astype(BF)
 
 
@@ -276,7 +274,7 @@
         functools.partial(send_body, n_dev),
         [
             pltpu.HBM((wide_rows, LANES), BF),
-            pltpu.HBM((count, 2 * t), BF),
+            pltpu.HBM((t, 2 * count), BF),
             pltpu.HBM((t, 8), F32),
             shape(w_in.shape[1:], BF),
             shape(w_out.shape[1:], BF),
@@ -284,7 +282,7 @@
         [expert_ids.T, gates.T, tokens, grad_out, w_in[0], w_out[0]],
         [
             pltpu.VMEM((wide_rows, LANES), BF),
-            pltpu.VMEM((count, 2 * t), BF),
+            pltpu.VMEM((t, 2 * count), BF),
             pltpu.VMEM((t, 8), F32),
             pltpu.VMEM((2, t), jnp.int32),
             pltpu.VMEM((2, t), F32),
@@ -349,22 +347,19 @@
         )
         other_half.append(lax.ppermute(own_half[h], "dp", cores))
 
-    def expert(hidden, upto):
-        so_far = []
-        for h in range(upto):
-            so_far = call(
-                functools.partial(rows_body, h),
-                [shape((n_core, 2 * width), F32)],
-                [hidden[h], *weights, *so_far],
-                (),
-                flops,
-            )
-        return so_far
+    own_rows, tokens, grad_out = call(
+        rows_body,
+        [shape((n_core, 2 * width), F32), shape((t, width), BF), shape((t, width), BF)],
+        [own_half[0], *weights, tokens, grad_out],
+        [pltpu.SemaphoreType.DMA((2,))],
+        flops,
+        (3, 4),
+    )
 
     (send_back,) = call(
         functools.partial(back_body, n_dev),
         [shape((wide_rows, LANES), BF)],
-        [me, other_half[-1], *expert(own_half, CHUNKS), *weights, *expert(other_half, CHUNKS - 1)],
+        [me, other_half[0], own_rows, *weights],
         [wide],
         flops,
     )
@@ -374,14 +369,8 @@
         functools.partial(combine_body, n_dev),
         [shape((t, width), BF), shape((t, width), BF)],
         [recv_back, picks, weigh, tokens, grad_out],
-        [
-            pltpu.VMEM((t, width), BF),
-            pltpu.VMEM((t, width), BF),
-            wide,
-            pltpu.SemaphoreType.DMA((2,)),
-        ],
+        [wide],
         2 * 3 * count * t * width,
-        (3, 4),
     )
     return moe_out, grad_tokens
 

time: 138 us -> 137 us (level)
  no operation moved by 1% of the time
where the time goes in v4:
time: 137 us
  waiting for transfers between devices  51.3 us (37%)
  starting transfers between devices  48.1 us (35%)
  blocking collectives  29.2 us (21%)
  Pallas kernels  7.76 us (6%)
    all_to_all x1, blocking collectives, exchange(): lax.all_to_all(parts, 'expert', split_axis=0, concat_axis=0, tiled=True)  29.2 us
    all_to_all x1, waiting for transfers between devices, exchange(): lax.all_to_all(parts, 'expert', split_axis=0, concat_axis=0, tiled=True)  27 us
    all_to_all x1, starting transfers between devices, exchange(): lax.all_to_all(parts, 'expert', split_axis=0, concat_axis=0, tiled=True)  22.4 us
    ppermute x1, waiting for transfers between devices, per_device(): from_half = lax.ppermute(to_half, 'dp', halves)  8.76 us
    pallas_call x10, Pallas kernels, call(): pl.pallas_call(body, out_shape=list(outs), in_specs=[SMEM if o.ndim == 1...  7.76 us
    ppermute x1, starting transfers between devices, per_device(): of_before = lax.ppermute(blocks[h], 'dp', after)  6.74 us
    ppermute x1, starting transfers between devices, per_device(): from_half = lax.ppermute(to_half, 'dp', halves)  6.67 us
    ppermute x1, waiting for transfers between devices, per_device(): of_after = lax.ppermute(blocks[h], 'dp', before)  5.43 us
  transfers between devices with their start and end apart: 8, of which 8 were waited for; matrix products, arithmetic and copies ran while one was open for 0% of the time, Pallas kernels for 1%

profile of v4, /device:TPU:64, one launch (start us, length us, event | category | flops | bytes accessed | tf_op | source)
XLA Modules:
  0.0 137.1 jit_solution(6661180402173741534)
XLA Ops:
  0.6 2.5 %shard_map.77 = (bf16[1536,128]{1,0:T(8,128)(2,1)}, bf16[256,384]{1,0:T(8,128)(2,1)}, f32[256,8]{1,0:T(8,128)}, bf16[512,2048]{1,0:T(8,128)(2,1)S(1)}, bf16[1024,512]{1,0:T(8,128)(2,1)S(1)}) custom-call(s32[2,256]{1,0:T(2,128)} %bitcast.15, f32[2,256]{1,0:T(2,128)} %bitcast.16, bf16[256,512]{1,0:T(8,128)(2,1)} %tokens_in.1, bf16[256,512]{1,0:T(8,128)(2,1)} %grad_in.1, ...), custom_call_target="tpu_custom_call" | custom-call | flops 109051904 | bytes 3674112 | tf_op jit(solution)/shard_map/pallas_call | solution.py:27
  3.1 22.4 %all-to-all-start = ((bf16[64,24,128]{2,1,0:T(8,128)(2,1)}), bf16[64,24,128]{2,1,0:T(8,128)(2,1)S(1)}, u32[]{:S(2)}, u32[]{:S(2)}) async-start(bf16[64,24,128]{2,1,0:T(8,128)(2,1)} %bitcast.14), calls=%async_computation | async-start | bytes 786432 | tf_op jit(solution)/shard_map/all_to_all | solution.py:301
  25.5 27.0 %all-to-all-done = bf16[64,24,128]{2,1,0:T(8,128)(2,1)S(1)} async-done(((bf16[64,24,128]{2,1,0:T(8,128)(2,1)}), bf16[64,24,128]{2,1,0:T(8,128)(2,1)S(1)}, u32[]{:S(2)}, u32[]{:S(2)}) %all-to-all-start) | async-done | bytes 393248 | tf_op jit(solution)/shard_map/all_to_all | solution.py:301
  52.5 0.8 shard_map.78
  53.3 1.9 %collective-permute-start = (bf16[96,3072]{1,0:T(8,128)(2,1)S(1)}, bf16[96,3072]{1,0:T(8,128)(2,1)S(1)}, u32[]{:S(2)}, u32[]{:S(2)}) collective-permute-start(bf16[96,3072]{1,0:T(8,128)(2,1)S(1)} %get-tuple-element.21), channel_id=1, source_target_pairs={{0,64},{64,0},{128,192},{192,128},{256,320},{320,256},{384,448},{4... | collective-permute-start | bytes 1769480 | tf_op jit(solution)/shard_map/ppermute | solution.py:323
  55.2 0.8 shard_map.79.mine
  56.0 1.2 collective-permute-done.from_core
  57.2 0.1 shard_map.80
  57.3 1.9 %collective-permute-start.1 = (bf16[32,3072]{1,0:T(8,128)(2,1)S(1)}, bf16[32,3072]{1,0:T(8,128)(2,1)S(1)}, u32[]{:S(2)}, u32[]{:S(2)}) collective-permute-start(bf16[32,3072]{1,0:T(8,128)(2,1)S(1)} %get-tuple-element.23), channel_id=1, source_target_pairs={{0,128},{64,192},{128,256},{192,320},{256,0},{320,64},{384,512},{4... | collective-permute-start | bytes 589832 | tf_op jit(solution)/shard_map/ppermute | solution.py:332
  59.3 3.9 %collective-permute-start.2 = (bf16[32,3072]{1,0:T(8,128)(2,1)S(1)}, bf16[32,3072]{1,0:T(8,128)(2,1)S(1)}, u32[]{:S(2)}, u32[]{:S(2)}) collective-permute-start(bf16[32,3072]{1,0:T(8,128)(2,1)S(1)} %get-tuple-element.24), channel_id=1, source_target_pairs={{0,256},{64,320},{128,0},{192,64},{256,128},{320,192},{384,640},{4... | collective-permute-start | bytes 589832 | tf_op jit(solution)/shard_map/ppermute | solution.py:333
  63.2 3.8 %collective-permute-done.1.from_before = bf16[32,3072]{1,0:T(8,128)(2,1)S(1)} collective-permute-done((bf16[32,3072]{1,0:T(8,128)(2,1)S(1)}, bf16[32,3072]{1,0:T(8,128)(2,1)S(1)}, u32[]{:S(2)}, u32[]{:S(2)}) %collective-permute-start.1) | collective-permute-done | bytes 196640 | tf_op jit(solution)/shard_map/ppermute | solution.py:332
  67.0 1.1 collective-permute-done.2.from_after
  68.1 0.1 shard_map.81
  68.2 6.7 %collective-permute-start.3 = (bf16[32,3072]{1,0:T(8,128)(2,1)S(1)}, bf16[32,3072]{1,0:T(8,128)(2,1)S(1)}, u32[]{:S(2)}, u32[]{:S(2)}) collective-permute-start(bf16[32,3072]{1,0:T(8,128)(2,1)S(1)} %get-tuple-element.26), channel_id=1, source_target_pairs={{0,384},{64,448},{128,512},{192,576},{256,640},{320,704},{384,0},{... | collective-permute-start | bytes 589832 | tf_op jit(solution)/shard_map/ppermute | solution.py:339
  74.9 8.8 %collective-permute-done.3.from_half = bf16[32,3072]{1,0:T(8,128)(2,1)S(1)} collective-permute-done((bf16[32,3072]{1,0:T(8,128)(2,1)S(1)}, bf16[32,3072]{1,0:T(8,128)(2,1)S(1)}, u32[]{:S(2)}, u32[]{:S(2)}) %collective-permute-start.3) | collective-permute-done | bytes 196640 | tf_op jit(solution)/shard_map/ppermute | solution.py:339
  83.6 0.1 shard_map.82.refs_0_
  83.7 6.7 %collective-permute-start.5 = (bf16[32,3072]{1,0:T(8,128)(2,1)S(1)}, bf16[32,3072]{1,0:T(8,128)(2,1)S(1)}, u32[]{:S(2)}, u32[]{:S(2)}) collective-permute-start(bf16[32,3072]{1,0:T(8,128)(2,1)S(1)} %shard_map.82.refs_0_), channel_id=1, source_target_pairs={{0,128},{64,192},{128,256},{192,320},{256,0},{320,64},{384,512},{4... | collective-permute-start | bytes 589832 | tf_op jit(solution)/shard_map/ppermute | solution.py:343
  90.5 2.7 %collective-permute-start.4 = (bf16[32,3072]{1,0:T(8,128)(2,1)S(1)}, bf16[32,3072]{1,0:T(8,128)(2,1)S(1)}, u32[]{:S(2)}, u32[]{:S(2)}) collective-permute-start(bf16[32,3072]{1,0:T(8,128)(2,1)S(1)} %shard_map.82.refs_0_), channel_id=1, source_target_pairs={{0,256},{64,320},{128,0},{192,64},{256,128},{320,192},{384,640},{4... | collective-permute-start | bytes 589832 | tf_op jit(solution)/shard_map/ppermute | solution.py:344
  93.1 3.1 %collective-permute-done.5.refs_2_ = bf16[32,3072]{1,0:T(8,128)(2,1)S(1)} collective-permute-done((bf16[32,3072]{1,0:T(8,128)(2,1)S(1)}, bf16[32,3072]{1,0:T(8,128)(2,1)S(1)}, u32[]{:S(2)}, u32[]{:S(2)}) %collective-permute-start.5) | collective-permute-done | bytes 196640 | tf_op jit(solution)/shard_map/ppermute | solution.py:343
  96.3 5.4 %collective-permute-done.4.refs_1_ = bf16[32,3072]{1,0:T(8,128)(2,1)S(1)} collective-permute-done((bf16[32,3072]{1,0:T(8,128)(2,1)S(1)}, bf16[32,3072]{1,0:T(8,128)(2,1)S(1)}, u32[]{:S(2)}, u32[]{:S(2)}) %collective-permute-start.4) | collective-permute-done | bytes 196640 | tf_op jit(solution)/shard_map/ppermute | solution.py:344
  101.7 1.9 %collective-permute-start.6 = (bf16[96,3072]{1,0:T(8,128)(2,1)S(1)}, bf16[96,3072]{1,0:T(8,128)(2,1)S(1)}, u32[]{:S(2)}, u32[]{:S(2)}) collective-permute-start(bf16[96,3072]{1,0:T(8,128)(2,1)S(1)} %shard_map.83.hidden), channel_id=1, source_target_pairs={{0,64},{64,0},{128,192},{192,128},{256,320},{320,256},{384,448},{4... | collective-permute-start | bytes 1769480 | tf_op jit(solution)/shard_map/ppermute | solution.py:348
  103.7 1.1 shard_map.84
  104.7 0.9 collective-permute-done.6.hidden
  105.6 0.0 copy-start
  105.6 0.0 copy-start.1
  105.6 1.0 shard_map.85
  106.7 29.2 %all_to_all.10 = bf16[64,24,128]{2,1,0:T(8,128)(2,1)S(1)} all-to-all(bf16[64,24,128]{2,1,0:T(8,128)(2,1)S(1)} %bitcast.10), channel_id=1, replica_groups=mesh['dp'=12,'expert'=64] {'expert'}, dimensions={0} | all-to-all | bytes 786432 | tf_op jit(solution)/shard_map/all_to_all | solution.py:301
  135.8 0.0 copy-done
  135.8 0.0 copy-done.1
  135.8 1.2 shard_map.86
  (1 shorter events, 0.0 us)
Async XLA Ops:
  3.1 49.3 %all-to-all-start = ((bf16[64,24,128]{2,1,0:T(8,128)(2,1)}), bf16[64,24,128]{2,1,0:T(8,128)(2,1)S(1)}, u32[]{:S(2)}, u32[]{:S(2)}) async-start(bf16[64,24,128]{2,1,0:T(8,128)(2,1)} %bitcast.14), calls=%async_computation | async-start | bytes 786432 | tf_op jit(solution)/shard_map/all_to_all | solution.py:301
  53.3 3.9 %collective-permute-start = (bf16[96,3072]{1,0:T(8,128)(2,1)S(1)}, bf16[96,3072]{1,0:T(8,128)(2,1)S(1)}, u32[]{:S(2)}, u32[]{:S(2)}) collective-permute-start(bf16[96,3072]{1,0:T(8,128)(2,1)S(1)} %get-tuple-element.21), channel_id=1, source_target_pairs={{0,64},{64,0},{128,192},{192,128},{256,320},{320,256},{384,448},{4... | collective-permute-start | bytes 1769480 | tf_op jit(solution)/shard_map/ppermute | solution.py:323
  57.3 9.6 %collective-permute-start.1 = (bf16[32,3072]{1,0:T(8,128)(2,1)S(1)}, bf16[32,3072]{1,0:T(8,128)(2,1)S(1)}, u32[]{:S(2)}, u32[]{:S(2)}) collective-permute-start(bf16[32,3072]{1,0:T(8,128)(2,1)S(1)} %get-tuple-element.23), channel_id=1, source_target_pairs={{0,128},{64,192},{128,256},{192,320},{256,0},{320,64},{384,512},{4... | collective-permute-start | bytes 589832 | tf_op jit(solution)/shard_map/ppermute | solution.py:332
  59.3 8.8 %collective-permute-start.2 = (bf16[32,3072]{1,0:T(8,128)(2,1)S(1)}, bf16[32,3072]{1,0:T(8,128)(2,1)S(1)}, u32[]{:S(2)}, u32[]{:S(2)}) collective-permute-start(bf16[32,3072]{1,0:T(8,128)(2,1)S(1)} %get-tuple-element.24), channel_id=1, source_target_pairs={{0,256},{64,320},{128,0},{192,64},{256,128},{320,192},{384,640},{4... | collective-permute-start | bytes 589832 | tf_op jit(solution)/shard_map/ppermute | solution.py:333
  68.2 15.4 %collective-permute-start.3 = (bf16[32,3072]{1,0:T(8,128)(2,1)S(1)}, bf16[32,3072]{1,0:T(8,128)(2,1)S(1)}, u32[]{:S(2)}, u32[]{:S(2)}) collective-permute-start(bf16[32,3072]{1,0:T(8,128)(2,1)S(1)} %get-tuple-element.26), channel_id=1, source_target_pairs={{0,384},{64,448},{128,512},{192,576},{256,640},{320,704},{384,0},{... | collective-permute-start | bytes 589832 | tf_op jit(solution)/shard_map/ppermute | solution.py:339
  83.7 12.6 %collective-permute-start.5 = (bf16[32,3072]{1,0:T(8,128)(2,1)S(1)}, bf16[32,3072]{1,0:T(8,128)(2,1)S(1)}, u32[]{:S(2)}, u32[]{:S(2)}) collective-permute-start(bf16[32,3072]{1,0:T(8,128)(2,1)S(1)} %shard_map.82.refs_0_), channel_id=1, source_target_pairs={{0,128},{64,192},{128,256},{192,320},{256,0},{320,64},{384,512},{4... | collective-permute-start | bytes 589832 | tf_op jit(solution)/shard_map/ppermute | solution.py:343
  90.5 11.2 %collective-permute-start.4 = (bf16[32,3072]{1,0:T(8,128)(2,1)S(1)}, bf16[32,3072]{1,0:T(8,128)(2,1)S(1)}, u32[]{:S(2)}, u32[]{:S(2)}) collective-permute-start(bf16[32,3072]{1,0:T(8,128)(2,1)S(1)} %shard_map.82.refs_0_), channel_id=1, source_target_pairs={{0,256},{64,320},{128,0},{192,64},{256,128},{320,192},{384,640},{4... | collective-permute-start | bytes 589832 | tf_op jit(solution)/shard_map/ppermute | solution.py:344
  101.7 3.9 %collective-permute-start.6 = (bf16[96,3072]{1,0:T(8,128)(2,1)S(1)}, bf16[96,3072]{1,0:T(8,128)(2,1)S(1)}, u32[]{:S(2)}, u32[]{:S(2)}) collective-permute-start(bf16[96,3072]{1,0:T(8,128)(2,1)S(1)} %shard_map.83.hidden), channel_id=1, source_target_pairs={{0,64},{64,0},{128,192},{192,128},{256,320},{320,256},{384,448},{4... | collective-permute-start | bytes 1769480 | tf_op jit(solution)/shard_map/ppermute | solution.py:348
  105.6 30.2 %copy-start = (bf16[256,384]{1,0:T(8,128)(2,1)S(1)}, bf16[256,384]{1,0:T(8,128)(2,1)}, u32[]{:S(2)}) copy-start(bf16[256,384]{1,0:T(8,128)(2,1)} %get-tuple-element.28.picks) | copy-start | bytes 589828
  105.6 30.2 %copy-start.1 = (f32[256,8]{1,0:T(8,128)S(1)}, f32[256,8]{1,0:T(8,128)}, u32[]{:S(2)}) copy-start(f32[256,8]{1,0:T(8,128)} %get-tuple-element.29.weigh) | copy-start | bytes 24580

commit v5 on v4

--- a/solution.py
+++ b/solution.py
@@ -9,7 +9,6 @@
 
 CAP = 3
 LANES = 128
-CHUNKS = 1
 BF = jnp.bfloat16
 F32 = jnp.float32
 VMEM = pl.BlockSpec(memory_space=pltpu.VMEM)
@@ -77,34 +76,30 @@
     return moves
 
 
-def send_body(n_dev, *refs):
-    send_out, picks_out, weigh_out, w_in, w_out, *rest = refs[6:]
-    send, picks, weigh, ids, gates, tokens, grad, wide, sems, out_sems = rest
-    moves = started(refs[:6], (ids, gates, tokens, grad, w_in, w_out), sems)
-    t, width = tokens.shape
+def one_hot(n_dev, ids):
+    t = ids.shape[1]
     expert = lax.broadcasted_iota(jnp.int32, (n_dev, t), 0)
+    hot = [jnp.where(expert == ids[k : k + 1, :], 1.0, 0.0) for k in range(2)]
     earlier = lax.broadcasted_iota(jnp.int32, (t, t), 0) < lax.broadcasted_iota(jnp.int32, (t, t), 1)
-    earlier = jnp.where(earlier, 1.0, 0.0).astype(BF)
-    moves[0].wait()
-    hot = [jnp.where(expert == ids[k : k + 1, :], 1.0, 0.0) for k in range(2)]
-    before = dot((hot[0] + hot[1]).astype(BF), earlier)
+    before = dot((hot[0] + hot[1]).astype(BF), jnp.where(earlier, 1.0, 0.0).astype(BF))
     before = [before, before + hot[0]]
-    picked = [
+    return [
         jnp.concatenate(
             [jnp.where(before[k] == float(j), hot[k], 0.0) for j in range(CAP)], axis=0
         )
         for k in range(2)
     ]
-    for k in range(2):
-        picks[:, k * CAP * n_dev : (k + 1) * CAP * n_dev] = picked[k].T.astype(BF)
-    outs = started((picks,), (picks_out,), out_sems)
+
+
+def send_body(n_dev, *refs):
+    send_out, ids, gates, tokens, grad, send, wide, sems, out_sems = refs[4:]
+    moves = started(refs[:4], (ids, gates, tokens, grad), sems)
+    width = tokens.shape[1]
+    moves[0].wait()
+    picked = one_hot(n_dev, ids)
     both = (picked[0] + picked[1]).astype(BF)
     moves[1].wait()
     gate = jnp.sum(picked[0] * gates[0:1, :] + picked[1] * gates[1:2, :], axis=1, keepdims=True)
-    copied = jnp.sum(jnp.where(ids[...] >= n_dev, gates[...], 0.0), axis=0, keepdims=True)
-    lines = [gates[...], copied, jnp.zeros((5, t), F32)]
-    weigh[...] = jnp.concatenate(lines, axis=0).T
-    outs += started((weigh,), (weigh_out,), out_sems.at[pl.ds(1, 1)])
     pieces = width // LANES
     stride = 2 * CAP * pieces
     for a in range(2):
@@ -116,21 +111,36 @@
                     j * n_dev : (j + 1) * n_dev, q * LANES : (q + 1) * LANES
                 ]
     part = wide.shape[0] // 4
+    outs = []
     for i in range(4):
         rows = pl.ds(i * part, part)
         send[rows, :] = wide[rows, :].astype(BF)
-        outs += started((send.at[rows],), (send_out.at[rows],), out_sems.at[pl.ds(2 + i, 1)])
-    for move in moves[4:] + outs:
+        outs += started((send.at[rows],), (send_out.at[rows],), out_sems.at[pl.ds(i, 1)])
+    for move in outs:
         move.wait()
 
 
-def product(out, rows_x, rows_g, w_in, w_out, chunk):
-    half = w_out.shape[0]
-    cut = half // CHUNKS
-    a = chunk * cut
-    out[:, :cut] = dot(rows_x, w_in[:, a : a + cut]).astype(BF)
-    out[:, cut : 2 * cut] = dot(rows_x, w_in[:, half + a : half + a + cut]).astype(BF)
-    out[:, 2 * cut :] = dot_t(rows_g, w_out[a : a + cut, :]).astype(BF)
+def ready_body(n_dev, *refs):
+    picks_out, weigh_out, w_in, w_out, picks, weigh, ids, gates, sems, out_sems = refs[4:]
+    moves = started(refs[:4], (ids, gates, w_in, w_out), sems)
+    t = ids.shape[1]
+    moves[0].wait()
+    count = CAP * n_dev
+    for k, picked in enumerate(one_hot(n_dev, ids)):
+        picks[:, k * count : (k + 1) * count] = picked.T.astype(BF)
+    outs = started((picks,), (picks_out,), out_sems)
+    moves[1].wait()
+    copied = jnp.sum(jnp.where(ids[...] >= n_dev, gates[...], 0.0), axis=0, keepdims=True)
+    weigh[...] = jnp.concatenate([gates[...], copied, jnp.zeros((5, t), F32)], axis=0).T
+    outs += started((weigh,), (weigh_out,), out_sems.at[pl.ds(1, 1)])
+    for move in moves[2:] + outs:
+        move.wait()
+
+
+def product(out, rows_x, rows_g, w_in, w_out):
+    cut = w_in.shape[1]
+    out[:, :cut] = dot(rows_x, w_in[...]).astype(BF)
+    out[:, cut:] = dot_t(rows_g, w_out[...]).astype(BF)
 
 
 def first_body(n_dev, me, recv, w_in, w_out, partial, rows, wide):
@@ -140,15 +150,14 @@
         rows[:, a * width : (a + 1) * width] = unpack(wide, a, n_dev, width).astype(BF)
     count = partial.shape[0]
     other = rows_at((1 - place_of(me)[0]) * count, count)
-    product(partial, rows[other, :width], rows[other, width:], w_in, w_out, 0)
-
-
-def part_body(own, chunk, me, rows, w_in, w_out, partial):
+    product(partial, rows[other, :width], rows[other, width:], w_in, w_out)
+
+
+def own_body(me, rows, w_in, w_out, partial):
     width = w_in.shape[0]
     count = partial.shape[0]
-    core = place_of(me)[0]
-    part = rows_at((core if own else 1 - core) * count, count)
-    product(partial, rows[part, :width], rows[part, width:], w_in, w_out, chunk)
+    own = rows_at(place_of(me)[0] * count, count)
+    product(partial, rows[own, :width], rows[own, width:], w_in, w_out)
 
 
 def third_body(me, mine, from_core, to_after, to_before, total):
@@ -190,32 +199,24 @@
         out[i * count : (i + 1) * count, :] = ref[...]
 
 
-def expert_rows(hidden, w_in, w_out, chunk):
+def expert_rows(hidden, w_in, w_out):
     half = w_out.shape[0]
-    cut = half // CHUNKS
-    a = chunk * cut
-    value = dot(hidden[:, :cut], w_out[a : a + cut, :])
-    grad = dot_t(hidden[:, cut : 2 * cut], w_in[:, a : a + cut])
-    grad = grad + dot_t(hidden[:, 2 * cut :], w_in[:, half + a : half + a + cut])
-    return value, grad
+    return dot(hidden[:, :half], w_out[...]), dot_t(hidden[:, half:], w_in[...])
 
 
 def rows_body(hidden, w_in, w_out, tokens_in, grad_in, out, tokens, grad_out, sems):
     moves = started((tokens_in, grad_in), (tokens, grad_out), sems)
     width = w_in.shape[0]
-    value, grad = expert_rows(hidden, w_in, w_out, 0)
+    value, grad = expert_rows(hidden, w_in, w_out)
     out[:, :width] = value
     out[:, width:] = grad
     for move in moves:
         move.wait()
 
 
-def back_body(n_dev, me, hidden, own_rows, w_in, w_out, *rest):
-    send, wide = rest[-2:]
+def back_body(n_dev, me, hidden, own_rows, w_in, w_out, send, wide):
     width = w_in.shape[0]
-    value, grad = expert_rows(hidden, w_in, w_out, CHUNKS - 1)
-    if CHUNKS > 1:
-        value, grad = rest[0][:, :width] + value, rest[0][:, width:] + grad
+    value, grad = expert_rows(hidden, w_in, w_out)
     core, _, chip = place_of(me)
     pieces = width // LANES
     stride = 2 * CAP * pieces
@@ -270,30 +271,41 @@
     after = [(i, i // 6 * 6 + (i + 2) % 6) for i in range(n_dp)]
     before = [(i, i // 6 * 6 + (i + 4) % 6) for i in range(n_dp)]
 
-    send, picks, weigh, *weights = call(
+    lines = [pltpu.VMEM((2, t), jnp.int32), pltpu.VMEM((2, t), F32)]
+    (send,) = call(
         functools.partial(send_body, n_dev),
+        [pltpu.HBM((wide_rows, LANES), BF)],
+        [expert_ids.T, gates.T, tokens, grad_out],
         [
-            pltpu.HBM((wide_rows, LANES), BF),
+            *lines,
+            pltpu.VMEM((t, width), BF),
+            pltpu.VMEM((t, width), BF),
+            pltpu.VMEM((wide_rows, LANES), BF),
+            wide,
+            pltpu.SemaphoreType.DMA((4,)),
+            pltpu.SemaphoreType.DMA((4,)),
+        ],
+        2 * (2 * count * t * width + n_dev * t * t),
+        range(4),
+    )
+    picks, weigh, *weights = call(
+        functools.partial(ready_body, n_dev),
+        [
             pltpu.HBM((t, 2 * count), BF),
             pltpu.HBM((t, 8), F32),
             shape(w_in.shape[1:], BF),
             shape(w_out.shape[1:], BF),
         ],
-        [expert_ids.T, gates.T, tokens, grad_out, w_in[0], w_out[0]],
+        [expert_ids.T, gates.T, w_in[0], w_out[0]],
         [
-            pltpu.VMEM((wide_rows, LANES), BF),
             pltpu.VMEM((t, 2 * count), BF),
             pltpu.VMEM((t, 8), F32),
-            pltpu.VMEM((2, t), jnp.int32),
-            pltpu.VMEM((2, t), F32),
-            pltpu.VMEM((t, width), BF),
-            pltpu.VMEM((t, width), BF),
-            wide,
-            pltpu.SemaphoreType.DMA((6,)),
-            pltpu.SemaphoreType.DMA((6,)),
+            *lines,
+            pltpu.SemaphoreType.DMA((4,)),
+            pltpu.SemaphoreType.DMA((2,)),
         ],
-        2 * (2 * count * t * width + n_dev * t * t),
-        range(6),
+        2 * n_dev * t * t,
+        range(4),
     )
 
     def exchange(rows):
@@ -303,10 +315,9 @@
 
     recv = exchange(send)
 
-    cw = 3 * half // CHUNKS
+    cw = 3 * half
     n_core, n_third = count // 2, count // 6
     flops = 2 * n_core * width * cw
-    chunks = range(CHUNKS)
     to_core, rows = call(
         functools.partial(first_body, n_dev),
         [shape((n_core, cw), BF), shape((count, 2 * width), BF)],
@@ -314,43 +325,26 @@
         [wide],
         flops,
     )
-
-    def part(own, chunk):
-        body = functools.partial(part_body, own, chunk)
-        return call(body, [shape((n_core, cw), BF)], [me, rows, *weights], (), flops)[0]
-
-    to_core = [to_core] + [part(False, h) for h in chunks[1:]]
-    from_core = [lax.ppermute(to_core[h], "dp", cores) for h in chunks]
-    mine = [part(True, h) for h in chunks]
-    blocks = []
-    for h in chunks:
-        to_after, to_before, total = call(
-            third_body,
-            [shape((n_third, cw), BF), shape((n_third, cw), BF), shape((n_third, cw), F32)],
-            [me, mine[h], from_core[h]],
-        )
-        from_before = lax.ppermute(to_after, "dp", after)
-        from_after = lax.ppermute(to_before, "dp", before)
-        to_half, total = call(
-            half_body,
-            [shape((n_third, cw), BF), shape((n_third, cw), F32)],
-            [total, from_before, from_after],
-        )
-        from_half = lax.ppermute(to_half, "dp", halves)
-        blocks.append(call(finish_body, [shape((n_third, cw), BF)], [total, from_half])[0])
-    own_half, other_half = [], []
-    for h in chunks:
-        of_before = lax.ppermute(blocks[h], "dp", after)
-        of_after = lax.ppermute(blocks[h], "dp", before)
-        own_half.append(
-            call(join_body, [shape((n_core, cw), BF)], [blocks[h], of_after, of_before])[0]
-        )
-        other_half.append(lax.ppermute(own_half[h], "dp", cores))
+    from_core = lax.ppermute(to_core, "dp", cores)
+    (mine,) = call(own_body, [shape((n_core, cw), BF)], [me, rows, *weights], (), flops)
+
+    third = shape((n_third, cw), BF)
+    wide_third = shape((n_third, cw), F32)
+    to_after, to_before, total = call(third_body, [third, third, wide_third], [me, mine, from_core])
+    from_before = lax.ppermute(to_after, "dp", after)
+    from_after = lax.ppermute(to_before, "dp", before)
+    to_half, total = call(half_body, [third, wide_third], [total, from_before, from_after])
+    from_half = lax.ppermute(to_half, "dp", halves)
+    (block,) = call(finish_body, [third], [total, from_half])
+    of_before = lax.ppermute(block, "dp", after)
+    of_after = lax.ppermute(block, "dp", before)
+    (own_half,) = call(join_body, [shape((n_core, cw), BF)], [block, of_after, of_before])
+    other_half = lax.ppermute(own_half, "dp", cores)
 
     own_rows, tokens, grad_out = call(
         rows_body,
         [shape((n_core, 2 * width), F32), shape((t, width), BF), shape((t, width), BF)],
-        [own_half[0], *weights, tokens, grad_out],
+        [own_half, *weights, tokens, grad_out],
         [pltpu.SemaphoreType.DMA((2,))],
         flops,
         (3, 4),
@@ -359,7 +353,7 @@
     (send_back,) = call(
         functools.partial(back_body, n_dev),
         [shape((wide_rows, LANES), BF)],
-        [me, other_half[0], own_rows, *weights],
+        [me, other_half, own_rows, *weights],
         [wide],
         flops,
     )

time: 137 us -> 137 us (level)
  waiting for transfers between devices: 51.3 us -> 49.3 us
  Pallas kernels: 7.76 us -> 9.46 us
    all_to_all x1, waiting for transfers between devices: 27 us -> 25 us  [exchange(): lax.all_to_all(parts, 'expert', split_axis=0, concat_axis=0, tiled=True)]
    pallas_call x10 -> x11, Pallas kernels: 7.76 us -> 9.46 us  [call(): pl.pallas_call(body, out_shape=list(outs), in_specs=[SMEM if o.ndim == 1...]
  transfers between devices with their start and end apart: 8 -> 8, of which waited for: 8 -> 8; matrix products, arithmetic and copies ran while one was open for 0% -> 0% of each run, Pallas kernels for 1% -> 3%
where the time goes in v5:
time: 137 us
  waiting for transfers between devices  49.3 us (36%)
  starting transfers between devices  48.1 us (35%)
  blocking collectives  29.2 us (21%)
  Pallas kernels  9.46 us (7%)
    all_to_all x1, blocking collectives, exchange(): lax.all_to_all(parts, 'expert', split_axis=0, concat_axis=0, tiled=True)  29.2 us
    all_to_all x1, waiting for transfers between devices, exchange(): lax.all_to_all(parts, 'expert', split_axis=0, concat_axis=0, tiled=True)  25 us
    all_to_all x1, starting transfers between devices, exchange(): lax.all_to_all(parts, 'expert', split_axis=0, concat_axis=0, tiled=True)  22.4 us
    pallas_call x11, Pallas kernels, call(): pl.pallas_call(body, out_shape=list(outs), in_specs=[SMEM if o.ndim == 1...  9.46 us
    ppermute x1, waiting for transfers between devices, per_device(): from_half = lax.ppermute(to_half, 'dp', halves)  8.76 us
    ppermute x1, starting transfers between devices, per_device(): of_before = lax.ppermute(block, 'dp', after)  6.74 us
    ppermute x1, starting transfers between devices, per_device(): from_half = lax.ppermute(to_half, 'dp', halves)  6.67 us
    ppermute x1, waiting for transfers between devices, per_device(): of_after = lax.ppermute(block, 'dp', before)  5.43 us
  transfers between devices with their start and end apart: 8, of which 8 were waited for; matrix products, arithmetic and copies ran while one was open for 0% of the time, Pallas kernels for 3%

profile of v5, /device:TPU:64, one launch (start us, length us, event | category | flops | bytes accessed | tf_op | source)
XLA Modules:
  0.0 136.8 jit_solution(7836387026936168669)
XLA Ops:
  0.6 2.3 %shard_map.77 = bf16[1536,128]{1,0:T(8,128)(2,1)} custom-call(s32[2,256]{1,0:T(2,128)} %bitcast.15, f32[2,256]{1,0:T(2,128)} %bitcast.17, bf16[256,512]{1,0:T(8,128)(2,1)} %tokens_in.1, bf16[256,512]{1,0:T(8,128)(2,1)} %grad_in.1), custom_call_target="tpu_custom_call" | custom-call | flops 109051904 | bytes 528384 | tf_op jit(solution)/shard_map/pallas_call | solution.py:26
  2.9 22.4 %all-to-all-start = ((bf16[64,24,128]{2,1,0:T(8,128)(2,1)}), bf16[64,24,128]{2,1,0:T(8,128)(2,1)S(1)}, u32[]{:S(2)}, u32[]{:S(2)}) async-start(bf16[64,24,128]{2,1,0:T(8,128)(2,1)} %bitcast.13), calls=%async_computation | async-start | bytes 786432 | tf_op jit(solution)/shard_map/all_to_all | solution.py:313
  25.3 1.9 %shard_map.78 = (bf16[256,384]{1,0:T(8,128)(2,1)}, f32[256,8]{1,0:T(8,128)}, bf16[512,2048]{1,0:T(8,128)(2,1)S(1)}, bf16[1024,512]{1,0:T(8,128)(2,1)S(1)}) custom-call(s32[2,256]{1,0:T(2,128)} %bitcast.16, f32[2,256]{1,0:T(2,128)} %bitcast.18, bf16[512,2048]{1,0:T(8,128)(2,1)} %bitcast.12, bf16[1024,512]{1,0:T(8,128)(2,1)} %bitcast.14), custom_call_target="tpu_custom_call" | custom-call | flops 8388608 | bytes 3149824 | tf_op jit(solution)/shard_map/pallas_call | solution.py:26
  27.2 25.0 %all-to-all-done = bf16[64,24,128]{2,1,0:T(8,128)(2,1)S(1)} async-done(((bf16[64,24,128]{2,1,0:T(8,128)(2,1)}), bf16[64,24,128]{2,1,0:T(8,128)(2,1)S(1)}, u32[]{:S(2)}, u32[]{:S(2)}) %all-to-all-start) | async-done | bytes 393248 | tf_op jit(solution)/shard_map/all_to_all | solution.py:313
  52.2 0.8 shard_map.79
  53.1 1.9 %collective-permute-start = (bf16[96,3072]{1,0:T(8,128)(2,1)S(1)}, bf16[96,3072]{1,0:T(8,128)(2,1)S(1)}, u32[]{:S(2)}, u32[]{:S(2)}) collective-permute-start(bf16[96,3072]{1,0:T(8,128)(2,1)S(1)} %get-tuple-element.19), channel_id=1, source_target_pairs={{0,64},{64,0},{128,192},{192,128},{256,320},{320,256},{384,448},{4... | collective-permute-start | bytes 1769480 | tf_op jit(solution)/shard_map/ppermute | solution.py:328
  55.0 0.8 shard_map.80.mine
  55.8 1.2 collective-permute-done.from_core
  57.0 0.1 shard_map.81
  57.1 1.9 %collective-permute-start.1 = (bf16[32,3072]{1,0:T(8,128)(2,1)S(1)}, bf16[32,3072]{1,0:T(8,128)(2,1)S(1)}, u32[]{:S(2)}, u32[]{:S(2)}) collective-permute-start(bf16[32,3072]{1,0:T(8,128)(2,1)S(1)} %get-tuple-element.21), channel_id=1, source_target_pairs={{0,128},{64,192},{128,256},{192,320},{256,0},{320,64},{384,512},{4... | collective-permute-start | bytes 589832 | tf_op jit(solution)/shard_map/ppermute | solution.py:334
  59.0 3.9 %collective-permute-start.2 = (bf16[32,3072]{1,0:T(8,128)(2,1)S(1)}, bf16[32,3072]{1,0:T(8,128)(2,1)S(1)}, u32[]{:S(2)}, u32[]{:S(2)}) collective-permute-start(bf16[32,3072]{1,0:T(8,128)(2,1)S(1)} %get-tuple-element.22), channel_id=1, source_target_pairs={{0,256},{64,320},{128,0},{192,64},{256,128},{320,192},{384,640},{4... | collective-permute-start | bytes 589832 | tf_op jit(solution)/shard_map/ppermute | solution.py:335
  63.0 3.8 %collective-permute-done.1.from_before = bf16[32,3072]{1,0:T(8,128)(2,1)S(1)} collective-permute-done((bf16[32,3072]{1,0:T(8,128)(2,1)S(1)}, bf16[32,3072]{1,0:T(8,128)(2,1)S(1)}, u32[]{:S(2)}, u32[]{:S(2)}) %collective-permute-start.1) | collective-permute-done | bytes 196640 | tf_op jit(solution)/shard_map/ppermute | solution.py:334
  66.7 1.1 collective-permute-done.2.from_after
  67.9 0.1 shard_map.82
  67.9 6.7 %collective-permute-start.3 = (bf16[32,3072]{1,0:T(8,128)(2,1)S(1)}, bf16[32,3072]{1,0:T(8,128)(2,1)S(1)}, u32[]{:S(2)}, u32[]{:S(2)}) collective-permute-start(bf16[32,3072]{1,0:T(8,128)(2,1)S(1)} %get-tuple-element.24), channel_id=1, source_target_pairs={{0,384},{64,448},{128,512},{192,576},{256,640},{320,704},{384,0},{... | collective-permute-start | bytes 589832 | tf_op jit(solution)/shard_map/ppermute | solution.py:337
  74.6 8.8 %collective-permute-done.3.from_half = bf16[32,3072]{1,0:T(8,128)(2,1)S(1)} collective-permute-done((bf16[32,3072]{1,0:T(8,128)(2,1)S(1)}, bf16[32,3072]{1,0:T(8,128)(2,1)S(1)}, u32[]{:S(2)}, u32[]{:S(2)}) %collective-permute-start.3) | collective-permute-done | bytes 196640 | tf_op jit(solution)/shard_map/ppermute | solution.py:337
  83.4 0.1 shard_map.83.refs_0_
  83.5 6.7 %collective-permute-start.5 = (bf16[32,3072]{1,0:T(8,128)(2,1)S(1)}, bf16[32,3072]{1,0:T(8,128)(2,1)S(1)}, u32[]{:S(2)}, u32[]{:S(2)}) collective-permute-start(bf16[32,3072]{1,0:T(8,128)(2,1)S(1)} %shard_map.83.refs_0_), channel_id=1, source_target_pairs={{0,128},{64,192},{128,256},{192,320},{256,0},{320,64},{384,512},{4... | collective-permute-start | bytes 589832 | tf_op jit(solution)/shard_map/ppermute | solution.py:339
  90.2 2.7 %collective-permute-start.4 = (bf16[32,3072]{1,0:T(8,128)(2,1)S(1)}, bf16[32,3072]{1,0:T(8,128)(2,1)S(1)}, u32[]{:S(2)}, u32[]{:S(2)}) collective-permute-start(bf16[32,3072]{1,0:T(8,128)(2,1)S(1)} %shard_map.83.refs_0_), channel_id=1, source_target_pairs={{0,256},{64,320},{128,0},{192,64},{256,128},{320,192},{384,640},{4... | collective-permute-start | bytes 589832 | tf_op jit(solution)/shard_map/ppermute | solution.py:340
  92.9 3.1 %collective-permute-done.5.refs_2_ = bf16[32,3072]{1,0:T(8,128)(2,1)S(1)} collective-permute-done((bf16[32,3072]{1,0:T(8,128)(2,1)S(1)}, bf16[32,3072]{1,0:T(8,128)(2,1)S(1)}, u32[]{:S(2)}, u32[]{:S(2)}) %collective-permute-start.5) | collective-permute-done | bytes 196640 | tf_op jit(solution)/shard_map/ppermute | solution.py:339
  96.0 5.4 %collective-permute-done.4.refs_1_ = bf16[32,3072]{1,0:T(8,128)(2,1)S(1)} collective-permute-done((bf16[32,3072]{1,0:T(8,128)(2,1)S(1)}, bf16[32,3072]{1,0:T(8,128)(2,1)S(1)}, u32[]{:S(2)}, u32[]{:S(2)}) %collective-permute-start.4) | collective-permute-done | bytes 196640 | tf_op jit(solution)/shard_map/ppermute | solution.py:340
  101.5 1.9 %collective-permute-start.6 = (bf16[96,3072]{1,0:T(8,128)(2,1)S(1)}, bf16[96,3072]{1,0:T(8,128)(2,1)S(1)}, u32[]{:S(2)}, u32[]{:S(2)}) collective-permute-start(bf16[96,3072]{1,0:T(8,128)(2,1)S(1)} %shard_map.84.hidden), channel_id=1, source_target_pairs={{0,64},{64,0},{128,192},{192,128},{256,320},{320,256},{384,448},{4... | collective-permute-start | bytes 1769480 | tf_op jit(solution)/shard_map/ppermute | solution.py:342
  103.4 1.1 shard_map.85
  104.5 0.9 collective-permute-done.6.hidden
  105.4 0.0 copy-start
  105.4 0.0 copy-start.1
  105.4 1.0 shard_map.86
  106.4 29.2 %all_to_all.10 = bf16[64,24,128]{2,1,0:T(8,128)(2,1)S(1)} all-to-all(bf16[64,24,128]{2,1,0:T(8,128)(2,1)S(1)} %bitcast.10), channel_id=1, replica_groups=mesh['dp'=12,'expert'=64] {'expert'}, dimensions={0} | all-to-all | bytes 786432 | tf_op jit(solution)/shard_map/all_to_all | solution.py:313
  135.6 0.0 copy-done
  135.6 0.0 copy-done.1
  135.6 1.2 shard_map.87
  (1 shorter events, 0.0 us)
Async XLA Ops:
  2.9 49.3 %all-to-all-start = ((bf16[64,24,128]{2,1,0:T(8,128)(2,1)}), bf16[64,24,128]{2,1,0:T(8,128)(2,1)S(1)}, u32[]{:S(2)}, u32[]{:S(2)}) async-start(bf16[64,24,128]{2,1,0:T(8,128)(2,1)} %bitcast.13), calls=%async_computation | async-start | bytes 786432 | tf_op jit(solution)/shard_map/all_to_all | solution.py:313
  53.1 3.9 %collective-permute-start = (bf16[96,3072]{1,0:T(8,128)(2,1)S(1)}, bf16[96,3072]{1,0:T(8,128)(2,1)S(1)}, u32[]{:S(2)}, u32[]{:S(2)}) collective-permute-start(bf16[96,3072]{1,0:T(8,128)(2,1)S(1)} %get-tuple-element.19), channel_id=1, source_target_pairs={{0,64},{64,0},{128,192},{192,128},{256,320},{320,256},{384,448},{4... | collective-permute-start | bytes 1769480 | tf_op jit(solution)/shard_map/ppermute | solution.py:328
  57.1 9.6 %collective-permute-start.1 = (bf16[32,3072]{1,0:T(8,128)(2,1)S(1)}, bf16[32,3072]{1,0:T(8,128)(2,1)S(1)}, u32[]{:S(2)}, u32[]{:S(2)}) collective-permute-start(bf16[32,3072]{1,0:T(8,128)(2,1)S(1)} %get-tuple-element.21), channel_id=1, source_target_pairs={{0,128},{64,192},{128,256},{192,320},{256,0},{320,64},{384,512},{4... | collective-permute-start | bytes 589832 | tf_op jit(solution)/shard_map/ppermute | solution.py:334
  59.0 8.8 %collective-permute-start.2 = (bf16[32,3072]{1,0:T(8,128)(2,1)S(1)}, bf16[32,3072]{1,0:T(8,128)(2,1)S(1)}, u32[]{:S(2)}, u32[]{:S(2)}) collective-permute-start(bf16[32,3072]{1,0:T(8,128)(2,1)S(1)} %get-tuple-element.22), channel_id=1, source_target_pairs={{0,256},{64,320},{128,0},{192,64},{256,128},{320,192},{384,640},{4... | collective-permute-start | bytes 589832 | tf_op jit(solution)/shard_map/ppermute | solution.py:335
  67.9 15.4 %collective-permute-start.3 = (bf16[32,3072]{1,0:T(8,128)(2,1)S(1)}, bf16[32,3072]{1,0:T(8,128)(2,1)S(1)}, u32[]{:S(2)}, u32[]{:S(2)}) collective-permute-start(bf16[32,3072]{1,0:T(8,128)(2,1)S(1)} %get-tuple-element.24), channel_id=1, source_target_pairs={{0,384},{64,448},{128,512},{192,576},{256,640},{320,704},{384,0},{... | collective-permute-start | bytes 589832 | tf_op jit(solution)/shard_map/ppermute | solution.py:337
  83.5 12.6 %collective-permute-start.5 = (bf16[32,3072]{1,0:T(8,128)(2,1)S(1)}, bf16[32,3072]{1,0:T(8,128)(2,1)S(1)}, u32[]{:S(2)}, u32[]{:S(2)}) collective-permute-start(bf16[32,3072]{1,0:T(8,128)(2,1)S(1)} %shard_map.83.refs_0_), channel_id=1, source_target_pairs={{0,128},{64,192},{128,256},{192,320},{256,0},{320,64},{384,512},{4... | collective-permute-start | bytes 589832 | tf_op jit(solution)/shard_map/ppermute | solution.py:339
  90.2 11.2 %collective-permute-start.4 = (bf16[32,3072]{1,0:T(8,128)(2,1)S(1)}, bf16[32,3072]{1,0:T(8,128)(2,1)S(1)}, u32[]{:S(2)}, u32[]{:S(2)}) collective-permute-start(bf16[32,3072]{1,0:T(8,128)(2,1)S(1)} %shard_map.83.refs_0_), channel_id=1, source_target_pairs={{0,256},{64,320},{128,0},{192,64},{256,128},{320,192},{384,640},{4... | collective-permute-start | bytes 589832 | tf_op jit(solution)/shard_map/ppermute | solution.py:340
  101.5 3.9 %collective-permute-start.6 = (bf16[96,3072]{1,0:T(8,128)(2,1)S(1)}, bf16[96,3072]{1,0:T(8,128)(2,1)S(1)}, u32[]{:S(2)}, u32[]{:S(2)}) collective-permute-start(bf16[96,3072]{1,0:T(8,128)(2,1)S(1)} %shard_map.84.hidden), channel_id=1, source_target_pairs={{0,64},{64,0},{128,192},{192,128},{256,320},{320,256},{384,448},{4... | collective-permute-start | bytes 1769480 | tf_op jit(solution)/shard_map/ppermute | solution.py:342
  105.4 30.2 %copy-start = (bf16[256,384]{1,0:T(8,128)(2,1)S(1)}, bf16[256,384]{1,0:T(8,128)(2,1)}, u32[]{:S(2)}) copy-start(bf16[256,384]{1,0:T(8,128)(2,1)} %get-tuple-element.26.picks) | copy-start | bytes 589828
  105.4 30.2 %copy-start.1 = (f32[256,8]{1,0:T(8,128)S(1)}, f32[256,8]{1,0:T(8,128)}, u32[]{:S(2)}) copy-start(f32[256,8]{1,0:T(8,128)} %get-tuple-element.27.weigh) | copy-start | bytes 24580

commit v6 on v5

--- a/solution.py
+++ b/solution.py
@@ -192,13 +192,6 @@
     block[:, 2 * cut :] = (hidden_grad * silu).astype(BF)
 
 
-def join_body(*refs):
-    out = refs[-1]
-    count = refs[0].shape[0]
-    for i, ref in enumerate(refs[:-1]):
-        out[i * count : (i + 1) * count, :] = ref[...]
-
-
 def expert_rows(hidden, w_in, w_out):
     half = w_out.shape[0]
     return dot(hidden[:, :half], w_out[...]), dot_t(hidden[:, half:], w_in[...])
@@ -217,15 +210,13 @@
 def back_body(n_dev, me, hidden, own_rows, w_in, w_out, send, wide):
     width = w_in.shape[0]
     value, grad = expert_rows(hidden, w_in, w_out)
-    core, _, chip = place_of(me)
+    core = place_of(me)[0]
     pieces = width // LANES
     stride = 2 * CAP * pieces
     count = hidden.shape[0] // 6
     for c in range(2):
         for i in range(6):
-            block = chip + i // 2
-            block = jnp.where(block >= 3, block - 3, block)
-            row = ((core ^ c) * 6 + block * 2 + i % 2) * count
+            row = ((core ^ c) * 6 + i) * count
             slot = row // n_dev
             start = (row - slot * n_dev) * stride + slot * pieces
             for a in range(2):
@@ -267,6 +258,7 @@
 
     me = lax.axis_index("dp").astype(jnp.int32).reshape(1)
     cores = [(i, i ^ 1) for i in range(n_dp)]
+    triples = [[h * 6 + c + 2 * i for i in range(3)] for h in range(2) for c in range(2)]
     halves = [(i, (i + 6) % n_dp) for i in range(n_dp)]
     after = [(i, i // 6 * 6 + (i + 2) % 6) for i in range(n_dp)]
     before = [(i, i // 6 * 6 + (i + 4) % 6) for i in range(n_dp)]
@@ -336,9 +328,7 @@
     to_half, total = call(half_body, [third, wide_third], [total, from_before, from_after])
     from_half = lax.ppermute(to_half, "dp", halves)
     (block,) = call(finish_body, [third], [total, from_half])
-    of_before = lax.ppermute(block, "dp", after)
-    of_after = lax.ppermute(block, "dp", before)
-    (own_half,) = call(join_body, [shape((n_core, cw), BF)], [block, of_after, of_before])
+    own_half = lax.all_gather(block, "dp", axis=0, tiled=True, axis_index_groups=triples)
     other_half = lax.ppermute(own_half, "dp", cores)
 
     own_rows, tokens, grad_out = call(

time: 137 us -> 137 us (level)
  the two profiles are of different devices: /device:TPU:64 before, /device:TPU:256 now
where the time goes in v6:
time: 137 us
  blocking collectives  49.8 us (36%)
  waiting for transfers between devices  44.9 us (33%)
  starting transfers between devices  32.1 us (23%)
  Pallas kernels  9.43 us (7%)
    all_to_all x1, blocking collectives, exchange(): lax.all_to_all(parts, 'expert', split_axis=0, concat_axis=0, tiled=True)  31.6 us
    all_to_all x1, waiting for transfers between devices, exchange(): lax.all_to_all(parts, 'expert', split_axis=0, concat_axis=0, tiled=True)  25.1 us
    all_to_all x1, starting transfers between devices, exchange(): lax.all_to_all(parts, 'expert', split_axis=0, concat_axis=0, tiled=True)  19 us
    all_gather x1, blocking collectives, per_device(): lax.all_gather(block, 'dp', axis=0, tiled=True, axis_index_groups=triples)  18.2 us
    ppermute x1, waiting for transfers between devices, per_device(): from_half = lax.ppermute(to_half, 'dp', halves)  13.2 us
    pallas_call x10, Pallas kernels, call(): pl.pallas_call(body, out_shape=list(outs), in_specs=[SMEM if o.ndim == 1...  9.43 us
    ppermute x1, starting transfers between devices, per_device(): from_after = lax.ppermute(to_before, 'dp', before)  5.13 us
    ppermute x1, waiting for transfers between devices, per_device(): from_before = lax.ppermute(to_after, 'dp', after)  3.78 us
  transfers between devices with their start and end apart: 6, of which 6 were waited for; matrix products, arithmetic and copies ran while one was open for 0% of the time, Pallas kernels for 3%

profile of v6, /device:TPU:256, one launch (start us, length us, event | category | flops | bytes accessed | tf_op | source)
XLA Modules:
  0.0 137.0 jit_solution(17318358768406973837)
XLA Ops:
  0.6 2.3 %shard_map.77 = bf16[1536,128]{1,0:T(8,128)(2,1)} custom-call(s32[2,256]{1,0:T(2,128)} %bitcast.15, f32[2,256]{1,0:T(2,128)} %bitcast.17, bf16[256,512]{1,0:T(8,128)(2,1)} %tokens_in.1, bf16[256,512]{1,0:T(8,128)(2,1)} %grad_in.1), custom_call_target="tpu_custom_call" | custom-call | flops 109051904 | bytes 528384 | tf_op jit(solution)/shard_map/pallas_call | solution.py:26
  2.9 19.0 %all-to-all-start = ((bf16[64,24,128]{2,1,0:T(8,128)(2,1)}), bf16[64,24,128]{2,1,0:T(8,128)(2,1)S(1)}, u32[]{:S(2)}, u32[]{:S(2)}) async-start(bf16[64,24,128]{2,1,0:T(8,128)(2,1)} %bitcast.13), calls=%async_computation | async-start | bytes 786432 | tf_op jit(solution)/shard_map/all_to_all | solution.py:305
  22.0 1.9 %shard_map.78 = (bf16[256,384]{1,0:T(8,128)(2,1)}, f32[256,8]{1,0:T(8,128)}, bf16[512,2048]{1,0:T(8,128)(2,1)S(1)}, bf16[1024,512]{1,0:T(8,128)(2,1)S(1)}) custom-call(s32[2,256]{1,0:T(2,128)} %bitcast.16, f32[2,256]{1,0:T(2,128)} %bitcast.18, bf16[512,2048]{1,0:T(8,128)(2,1)} %bitcast.12, bf16[1024,512]{1,0:T(8,128)(2,1)} %bitcast.14), custom_call_target="tpu_custom_call" | custom-call | flops 8388608 | bytes 3149824 | tf_op jit(solution)/shard_map/pallas_call | solution.py:26
  23.9 25.1 %all-to-all-done = bf16[64,24,128]{2,1,0:T(8,128)(2,1)S(1)} async-done(((bf16[64,24,128]{2,1,0:T(8,128)(2,1)}), bf16[64,24,128]{2,1,0:T(8,128)(2,1)S(1)}, u32[]{:S(2)}, u32[]{:S(2)}) %all-to-all-start) | async-done | bytes 393248 | tf_op jit(solution)/shard_map/all_to_all | solution.py:305
  49.0 0.9 shard_map.79
  49.9 1.9 %collective-permute-start = (bf16[96,3072]{1,0:T(8,128)(2,1)S(1)}, bf16[96,3072]{1,0:T(8,128)(2,1)S(1)}, u32[]{:S(2)}, u32[]{:S(2)}) collective-permute-start(bf16[96,3072]{1,0:T(8,128)(2,1)S(1)} %get-tuple-element.19), channel_id=1, source_target_pairs={{0,64},{64,0},{128,192},{192,128},{256,320},{320,256},{384,448},{4... | collective-permute-start | bytes 1769480 | tf_op jit(solution)/shard_map/ppermute | solution.py:320
  51.8 0.8 shard_map.80.mine
  52.6 1.2 collective-permute-done.from_core
  53.8 0.1 shard_map.81
  53.9 1.9 %collective-permute-start.1 = (bf16[32,3072]{1,0:T(8,128)(2,1)S(1)}, bf16[32,3072]{1,0:T(8,128)(2,1)S(1)}, u32[]{:S(2)}, u32[]{:S(2)}) collective-permute-start(bf16[32,3072]{1,0:T(8,128)(2,1)S(1)} %get-tuple-element.21), channel_id=1, source_target_pairs={{0,128},{64,192},{128,256},{192,320},{256,0},{320,64},{384,512},{4... | collective-permute-start | bytes 589832 | tf_op jit(solution)/shard_map/ppermute | solution.py:326
  55.8 5.1 %collective-permute-start.2 = (bf16[32,3072]{1,0:T(8,128)(2,1)S(1)}, bf16[32,3072]{1,0:T(8,128)(2,1)S(1)}, u32[]{:S(2)}, u32[]{:S(2)}) collective-permute-start(bf16[32,3072]{1,0:T(8,128)(2,1)S(1)} %get-tuple-element.22), channel_id=1, source_target_pairs={{0,256},{64,320},{128,0},{192,64},{256,128},{320,192},{384,640},{4... | collective-permute-start | bytes 589832 | tf_op jit(solution)/shard_map/ppermute | solution.py:327
  61.0 3.8 %collective-permute-done.1.from_before = bf16[32,3072]{1,0:T(8,128)(2,1)S(1)} collective-permute-done((bf16[32,3072]{1,0:T(8,128)(2,1)S(1)}, bf16[32,3072]{1,0:T(8,128)(2,1)S(1)}, u32[]{:S(2)}, u32[]{:S(2)}) %collective-permute-start.1) | collective-permute-done | bytes 196640 | tf_op jit(solution)/shard_map/ppermute | solution.py:326
  64.7 0.7 collective-permute-done.2.from_after
  65.4 0.1 shard_map.82
  65.5 2.2 %collective-permute-start.3 = (bf16[32,3072]{1,0:T(8,128)(2,1)S(1)}, bf16[32,3072]{1,0:T(8,128)(2,1)S(1)}, u32[]{:S(2)}, u32[]{:S(2)}) collective-permute-start(bf16[32,3072]{1,0:T(8,128)(2,1)S(1)} %get-tuple-element.24), channel_id=1, source_target_pairs={{0,384},{64,448},{128,512},{192,576},{256,640},{320,704},{384,0},{... | collective-permute-start | bytes 589832 | tf_op jit(solution)/shard_map/ppermute | solution.py:329
  67.7 13.2 %collective-permute-done.3.from_half = bf16[32,3072]{1,0:T(8,128)(2,1)S(1)} collective-permute-done((bf16[32,3072]{1,0:T(8,128)(2,1)S(1)}, bf16[32,3072]{1,0:T(8,128)(2,1)S(1)}, u32[]{:S(2)}, u32[]{:S(2)}) %collective-permute-start.3) | collective-permute-done | bytes 196640 | tf_op jit(solution)/shard_map/ppermute | solution.py:329
  80.9 0.1 shard_map.83
  81.0 18.2 %all_gather.3.hidden = bf16[96,3072]{1,0:T(8,128)(2,1)S(1)} all-gather(bf16[32,3072]{1,0:T(8,128)(2,1)S(1)} %shard_map.83), channel_id=1, replica_groups={{0,128,256},{64,192,320},{384,512,640},{448,576,704},{1,129,257},{65,19..., dimensions={0}, use_global_device_ids=true | all-gather | bytes 786432 | tf_op jit(solution)/shard_map/all_gather | solution.py:331
  99.2 1.9 %collective-permute-start.4 = (bf16[96,3072]{1,0:T(8,128)(2,1)S(1)}, bf16[96,3072]{1,0:T(8,128)(2,1)S(1)}, u32[]{:S(2)}, u32[]{:S(2)}) collective-permute-start(bf16[96,3072]{1,0:T(8,128)(2,1)S(1)} %all_gather.3.hidden), channel_id=1, source_target_pairs={{0,64},{64,0},{128,192},{192,128},{256,320},{320,256},{384,448},{4... | collective-permute-start | bytes 1769480 | tf_op jit(solution)/shard_map/ppermute | solution.py:332
  101.1 1.1 shard_map.84
  102.2 0.9 collective-permute-done.4.hidden
  103.1 0.0 copy-start
  103.1 0.0 copy-start.1
  103.1 1.0 shard_map.85
  104.1 31.6 %all_to_all.10 = bf16[64,24,128]{2,1,0:T(8,128)(2,1)S(1)} all-to-all(bf16[64,24,128]{2,1,0:T(8,128)(2,1)S(1)} %bitcast.10), channel_id=1, replica_groups=mesh['dp'=12,'expert'=64] {'expert'}, dimensions={0} | all-to-all | bytes 786432 | tf_op jit(solution)/shard_map/all_to_all | solution.py:305
  135.7 0.0 copy-done
  135.7 0.0 copy-done.1
  135.7 1.2 shard_map.86
Async XLA Ops:
  2.9 46.1 %all-to-all-start = ((bf16[64,24,128]{2,1,0:T(8,128)(2,1)}), bf16[64,24,128]{2,1,0:T(8,128)(2,1)S(1)}, u32[]{:S(2)}, u32[]{:S(2)}) async-start(bf16[64,24,128]{2,1,0:T(8,128)(2,1)} %bitcast.13), calls=%async_computation | async-start | bytes 786432 | tf_op jit(solution)/shard_map/all_to_all | solution.py:305
  49.9 3.9 %collective-permute-start = (bf16[96,3072]{1,0:T(8,128)(2,1)S(1)}, bf16[96,3072]{1,0:T(8,128)(2,1)S(1)}, u32[]{:S(2)}, u32[]{:S(2)}) collective-permute-start(bf16[96,3072]{1,0:T(8,128)(2,1)S(1)} %get-tuple-element.19), channel_id=1, source_target_pairs={{0,64},{64,0},{128,192},{192,128},{256,320},{320,256},{384,448},{4... | collective-permute-start | bytes 1769480 | tf_op jit(solution)/shard_map/ppermute | solution.py:320
  53.9 10.8 %collective-permute-start.1 = (bf16[32,3072]{1,0:T(8,128)(2,1)S(1)}, bf16[32,3072]{1,0:T(8,128)(2,1)S(1)}, u32[]{:S(2)}, u32[]{:S(2)}) collective-permute-start(bf16[32,3072]{1,0:T(8,128)(2,1)S(1)} %get-tuple-element.21), channel_id=1, source_target_pairs={{0,128},{64,192},{128,256},{192,320},{256,0},{320,64},{384,512},{4... | collective-permute-start | bytes 589832 | tf_op jit(solution)/shard_map/ppermute | solution.py:326
  55.8 9.6 %collective-permute-start.2 = (bf16[32,3072]{1,0:T(8,128)(2,1)S(1)}, bf16[32,3072]{1,0:T(8,128)(2,1)S(1)}, u32[]{:S(2)}, u32[]{:S(2)}) collective-permute-start(bf16[32,3072]{1,0:T(8,128)(2,1)S(1)} %get-tuple-element.22), channel_id=1, source_target_pairs={{0,256},{64,320},{128,0},{192,64},{256,128},{320,192},{384,640},{4... | collective-permute-start | bytes 589832 | tf_op jit(solution)/shard_map/ppermute | solution.py:327
  65.5 15.4 %collective-permute-start.3 = (bf16[32,3072]{1,0:T(8,128)(2,1)S(1)}, bf16[32,3072]{1,0:T(8,128)(2,1)S(1)}, u32[]{:S(2)}, u32[]{:S(2)}) collective-permute-start(bf16[32,3072]{1,0:T(8,128)(2,1)S(1)} %get-tuple-element.24), channel_id=1, source_target_pairs={{0,384},{64,448},{128,512},{192,576},{256,640},{320,704},{384,0},{... | collective-permute-start | bytes 589832 | tf_op jit(solution)/shard_map/ppermute | solution.py:329
  99.2 3.9 %collective-permute-start.4 = (bf16[96,3072]{1,0:T(8,128)(2,1)S(1)}, bf16[96,3072]{1,0:T(8,128)(2,1)S(1)}, u32[]{:S(2)}, u32[]{:S(2)}) collective-permute-start(bf16[96,3072]{1,0:T(8,128)(2,1)S(1)} %all_gather.3.hidden), channel_id=1, source_target_pairs={{0,64},{64,0},{128,192},{192,128},{256,320},{320,256},{384,448},{4... | collective-permute-start | bytes 1769480 | tf_op jit(solution)/shard_map/ppermute | solution.py:332
  103.1 32.6 %copy-start = (bf16[256,384]{1,0:T(8,128)(2,1)S(1)}, bf16[256,384]{1,0:T(8,128)(2,1)}, u32[]{:S(2)}) copy-start(bf16[256,384]{1,0:T(8,128)(2,1)} %get-tuple-element.26.picks) | copy-start | bytes 589828
  103.1 32.6 %copy-start.1 = (f32[256,8]{1,0:T(8,128)S(1)}, f32[256,8]{1,0:T(8,128)}, u32[]{:S(2)}) copy-start(f32[256,8]{1,0:T(8,128)} %get-tuple-element.27.weigh) | copy-start | bytes 24580
